TPU v7x, 32 devices: a whole 2x2x4 slice. The times are simulated.
32 devices in a mesh: region: 4 (over z), slab: 8 (over y, x, core).
Axes of the slice: x: 2, y: 2, z: 4, core: 2. Of those that a mesh axis runs over, the one named last changes fastest.
Arguments:
- records: bfloat16 [1024, 4096], P('region', 'slab'), may hold values from -6 to 6
- first_station: int32 [4096], P(('region', 'slab')), may hold values from 0 to 255
- second_region: int32 [4096, 1], P(('region', 'slab')), may hold values from 0 to 3; in each aligned block of 128 rows (0 to 127, 128 to 255, ...) at most 40 rows name the same one
- second_station: int32 [4096], P(('region', 'slab')), may hold values from 0 to 255
Outputs:
- stacks: bfloat16 [4096, 2048], P(('region', 'slab'))
Inputs may be any that keep to these rules, and one draw needn't show every extreme that they name: `second_region`: no region is named by more than 40 pairs of one device.
All inputs are finite; a program needn't handle non-finite values.
Results may differ from a plain program's by a relative error of at most 0.0077.
Values may be sent and summed in bfloat16 or wider, within the bound.
No kernel may reach another device: no remote copies, remote signals or barrier semaphores. Data moves between devices by JAX's collectives and lax.ppermute only.
A program may use at most 64 MiB of HBM per device.

v0:
```python
import math

import jax
import jax.numpy as jnp
from jax import lax
from jax.sharding import PartitionSpec as P

NFFT = 2048
BINS = 1024
SEG = 2
HALF = 4


def dft_table():
    sample = jnp.arange(NFFT, dtype=jnp.int32)[:, None]
    frequency = jnp.arange(BINS, dtype=jnp.int32)[None, :]
    phase = (sample * frequency % NFFT).astype(jnp.float32) * (2.0 * math.pi / NFFT)
    return jnp.concatenate([jnp.cos(phase), -jnp.sin(phase)], axis=1).astype(jnp.bfloat16)


def whitened(traces):
    count = traces.shape[0]
    signal = traces.astype(jnp.float32).reshape(count * SEG, NFFT)
    signal = signal - jnp.mean(signal, axis=1, keepdims=True)
    position = jnp.arange(NFFT, dtype=jnp.int32).astype(jnp.float32)
    taper = 0.5 - 0.5 * jnp.cos(position * (2.0 * math.pi / NFFT))
    tapered = (signal * taper[None, :]).astype(jnp.bfloat16)
    spectrum = jnp.dot(tapered, dft_table(), preferred_element_type=jnp.float32)
    real_part = spectrum[:, :BINS]
    imag_part = spectrum[:, BINS:]
    amplitude = jnp.sqrt(real_part * real_part + imag_part * imag_part + 1e-06)
    padded = jnp.pad(amplitude, ((0, 0), (HALF, HALF)))
    smooth = jnp.zeros_like(amplitude)
    for offset in range(2 * HALF + 1):
        smooth = smooth + padded[:, offset : offset + BINS]
    smooth = smooth / (2 * HALF + 1)
    level = jnp.mean(amplitude, axis=1, keepdims=True)
    divisor = smooth + level + 1e-06
    white = spectrum / jnp.concatenate([divisor, divisor], axis=1)
    return white.astype(jnp.bfloat16).reshape(count, SEG * NFFT)


def cross(first_rows, second_rows):
    left = first_rows.astype(jnp.float32).reshape(first_rows.shape[:-1] + (SEG, 2, BINS))
    right = second_rows.astype(jnp.float32).reshape(second_rows.shape[:-1] + (SEG, 2, BINS))
    real_sum = jnp.mean(
        left[..., 0, :] * right[..., 0, :] + left[..., 1, :] * right[..., 1, :], axis=-2
    )
    imag_sum = jnp.mean(
        left[..., 0, :] * right[..., 1, :] - left[..., 1, :] * right[..., 0, :], axis=-2
    )
    return jnp.concatenate([real_sum, imag_sum], axis=-1).astype(jnp.bfloat16)


def local(records, first_station, second_region, second_station):
    regions = lax.axis_size("region")
    pair_count = first_station.shape[0]
    capacity = max(2, pair_count // regions + pair_count // 16)
    arrived = lax.all_to_all(records, "slab", split_axis=0, concat_axis=1, tiled=True)
    spectra = whitened(arrived)
    width = spectra.shape[1]
    target = second_region[:, 0]
    onehot = (target[:, None] == jnp.arange(regions, dtype=jnp.int32)[None, :]).astype(jnp.int32)
    ranking = jnp.sum((jnp.cumsum(onehot, axis=0) - onehot) * onehot, axis=1)
    slot_index = target * capacity + ranking
    requests = (
        jnp.zeros((regions * capacity,), jnp.int32)
        .at[slot_index]
        .set(second_station)
        .reshape(regions, capacity)
    )
    incoming = lax.all_to_all(requests, "region", split_axis=0, concat_axis=0, tiled=True)
    wanted = jnp.concatenate([first_station, incoming.reshape(-1)])
    initial = jnp.zeros((wanted.shape[0], width), jnp.bfloat16)
    piece = lax.all_gather(spectra, "slab", axis=0, tiled=True)
    inside = (wanted >= 0) & (wanted < piece.shape[0])
    chosen = jnp.take(piece, jnp.clip(wanted, 0, piece.shape[0] - 1), axis=0)
    picked = jnp.where(inside[:, None], chosen, initial)
    first_rows = picked[:pair_count]
    served = picked[pair_count:]
    returned = lax.all_to_all(
        served.reshape(regions, capacity, width), "region", split_axis=0, concat_axis=0, tiled=True
    )
    second_rows = jnp.take(returned.reshape(regions * capacity, width), slot_index, axis=0)
    stacks = cross(first_rows, second_rows)
    return stacks


def solution(mesh):
    placed = (
        P("region", "slab"),
        P(("region", "slab")),
        P(("region", "slab"), None),
        P(("region", "slab")),
    )
    return jax.shard_map(
        local, mesh=mesh, in_specs=placed, out_specs=P(("region", "slab"), None), check_vma=False
    )
```

profile of v0, /device:TPU:1, one launch (start us, length us, event | category | flops | bytes accessed | tf_op | source)
XLA Modules:
  0.0 149.6 jit_solution(5005157133160805071)
XLA Ops:
  6.5 5.2 %all-to-all-start.1 = ((bf16[8,32,512]{2,1,0:T(8,128)(2,1)}), bf16[8,32,512]{2,1,0:T(8,128)(2,1)S(1)}, u32[]{:S(2)}, u32[]{:S(2)}) async-start(bf16[8,32,512]{2,1,0:T(8,128)(2,1)} %bitcast.19), calls=%async_computation.1 | async-start | bytes 524288 | tf_op jit(solution)/shard_map/all_to_all | solution.py:59
  11.8 0.0 all-gather.2.cloned.1.call-start
  11.8 34.9 %negate_convert_fusion = (bf16[2048,1024]{1,0:T(8,128)(2,1)}, bf16[2048,1024]{1,0:T(8,128)(2,1)}) fusion(), kind=kLoop, calls=%fused_computation.13 | loop fusion | flops 35651584 | bytes 8388608 | tf_op jit(solution)/shard_map/convert.6
  46.7 0.1 multiply_subtract_fusion
  46.8 0.0 all-to-all-done.1
  46.8 0.1 convert_reduce_fusion
  46.9 0.1 copy.8
  47.0 0.1 reduce_sum.60
  47.0 0.1 reduce_sum.61
  47.2 0.1 convert_bitcast_fusion
  47.2 0.3 copy.7
  47.5 0.2 reshape.149
  47.8 0.0 copy-start.1
  47.8 0.0 copy-start.2
  47.8 4.4 %fusion.3 = f32[64,2048]{1,0:T(8,128)S(1)} fusion(bf16[2048,1024]{1,0:T(8,128)(2,1)} %get-tuple-element.13, bf16[2048,1024]{1,0:T(8,128)(2,1)} %get-tuple-element.14, f32[64,2048]{1,0:T(8,128)S(1)} %reshape.149, f32[2048]{0:T(1024)S(1)} %multiply_subtract_fusion, f32[64]{0:T(128)S(1)} %broadcast_multiply_fusion.1), kind=kOutput, calls=%fused_computation.9 | convolution fusion | flops 554041344 | bytes 9445632 | tf_op jit(solution)/shard_map/dot_general | solution.py:28
  52.2 0.2 fusion.33
  52.4 0.6 fusion.22
  53.1 0.1 fusion.11
  53.1 0.8 reshape.144
  53.9 0.0 all-gather.2.cloned.1.call-update
  53.9 0.0 copy-done.1
  53.9 0.1 fusion.28
  54.0 0.2 reduce_window_sum.11
  54.2 0.2 select_reduce_fusion
  54.4 1.1 scatter_custom_fusion
  55.5 0.7 all_to_all.19
  56.2 4.6 %all-to-all-start = ((s32[4,1,40]{2,1,0:T(1,128)}), s32[4,1,40]{2,1,0:T(1,128)S(1)}, u32[]{:S(2)}, u32[]{:S(2)}) async-start(s32[4,1,40]{2,1,0:T(1,128)} %all_to_all.19), calls=%async_computation | async-start | bytes 4096 | tf_op jit(solution)/shard_map/all_to_all | solution.py:72
  60.8 0.0 copy-done.2
  60.8 4.2 %all-to-all-done = s32[4,1,40]{2,1,0:T(1,128)S(1)} async-done(((s32[4,1,40]{2,1,0:T(1,128)}), s32[4,1,40]{2,1,0:T(1,128)S(1)}, u32[]{:S(2)}, u32[]{:S(2)}) %all-to-all-start) | async-done | bytes 672 | tf_op jit(solution)/shard_map/all_to_all | solution.py:72
  65.0 0.1 concatenate.43
  65.1 0.5 broadcast.142
  65.6 0.6 reduce.12
  66.3 0.1 concatenate.38
  66.4 17.0 %all-gather.2.cloned.1.call-done = bf16[256,4096]{1,0:T(8,128)(2,1)} async-done(((bf16[32,4096]{1,0:T(8,128)(2,1)}), bf16[256,4096]{1,0:T(8,128)(2,1)}) %all-gather.2.cloned.1.call-update) | async-done | bytes 2097168 | tf_op jit(solution)/shard_map/all_gather | solution.py:75
  83.5 9.3 %gather_fusion = bf16[288,4096]{1,0:T(8,128)(2,1)S(1)} fusion(bf16[256,4096]{1,0:T(8,128)(2,1)} %all-gather.2.cloned.1.call-done, s32[1024]{0:T(1024)S(1)} %pad_clamp_fusion.1), kind=kCustom, calls=%fused_computation | custom fusion | bytes 4719744 | tf_op jit(solution)/shard_map/jit(_take)/gather | solution.py:77
  92.8 0.4 select_select_fusion
  93.2 0.0 copy-start
  93.2 1.4 copy-done
  94.6 1.2 slice.77
  95.8 4.3 %all-to-all-start.2 = ((bf16[4,40,4096]{2,1,0:T(8,128)(2,1)}), bf16[4,40,4096]{2,1,0:T(8,128)(2,1)S(1)}, u32[]{:S(2)}, u32[]{:S(2)}) async-start(bf16[4,40,4096]{2,1,0:T(8,128)(2,1)} %bitcast.8), calls=%async_computation.2 | async-start | bytes 2621440 | tf_op jit(solution)/shard_map/all_to_all | solution.py:81
  100.2 2.8 %slice_convert_fusion = f32[128,4096]{1,0:T(8,128)} fusion(bf16[288,4096]{1,0:T(8,128)(2,1)} %copy-done), kind=kLoop, calls=%fused_computation.21 | loop fusion | flops 524288 | bytes 3145728 | tf_op jit(solution)/shard_map/reshape | solution.py:44
  102.9 3.0 %reshape.151 = f32[128,2,2,1024]{3,2,1,0:T(2,128)S(1)} reshape(f32[128,4096]{1,0:T(8,128)} %slice_convert_fusion) | data formatting | bytes 4194304 | tf_op jit(solution)/shard_map/reshape | solution.py:44
  105.9 25.1 %all-to-all-done.2 = bf16[4,40,4096]{2,1,0:T(8,128)(2,1)S(1)} async-done(((bf16[4,40,4096]{2,1,0:T(8,128)(2,1)}), bf16[4,40,4096]{2,1,0:T(8,128)(2,1)S(1)}, u32[]{:S(2)}, u32[]{:S(2)}) %all-to-all-start.2) | async-done | bytes 1310752 | tf_op jit(solution)/shard_map/all_to_all | solution.py:81
  131.1 2.2 %gather_fusion.1 = bf16[128,4096]{1,0:T(8,128)(2,1)} fusion(bf16[160,4096]{1,0:T(8,128)(2,1)S(1)} %bitcast.18, s32[1024]{0:T(1024)S(1)} %pad_clamp_fusion), kind=kCustom, calls=%fused_computation.1 | custom fusion | bytes 2097664 | tf_op jit(solution)/shard_map/jit(_take)/gather | solution.py:84
  133.3 1.8 %gather.12 = bf16[128,2,2,1024]{3,2,1,0:T(2,128)(2,1)S(1)} reshape(bf16[128,4096]{1,0:T(8,128)(2,1)} %gather_fusion.1) | data formatting | bytes 2097152 | tf_op jit(solution)/shard_map/jit(_take)/gather | solution.py:84
  135.1 1.0 fusion.10
  136.1 5.8 %add_reduce_fusion = (f32[128,1024]{1,0:T(8,128)S(1)}, f32[128,1024]{1,0:T(8,128)S(1)}) fusion(f32[128,2,2,1024]{3,2,1,0:T(2,128)S(1)} %fusion.10, f32[128,2,2,1024]{3,2,1,0:T(2,128)S(1)} %reshape.151), kind=kLoop, calls=%fused_computation.23 | loop fusion | flops 1835008 | bytes 5242880 | tf_op jit(solution)/shard_map/reduce_sum | solution.py:46
  142.0 0.8 pad_maximum_fusion
  (12 shorter events, 0.2 us)
Async XLA Ops:
  6.5 40.2 %all-to-all-start.1 = ((bf16[8,32,512]{2,1,0:T(8,128)(2,1)}), bf16[8,32,512]{2,1,0:T(8,128)(2,1)S(1)}, u32[]{:S(2)}, u32[]{:S(2)}) async-start(bf16[8,32,512]{2,1,0:T(8,128)(2,1)} %bitcast.19), calls=%async_computation.1 | async-start | bytes 524288 | tf_op jit(solution)/shard_map/all_to_all | solution.py:59
  11.8 71.7 %all-gather.2.cloned.1.call-start = ((), (), s32[]{:S(2)}) async-start(), calls=%async_computation.3 | async-start | bytes 2359296 | tf_op jit(solution)/shard_map/all_gather | solution.py:75
  47.8 6.2 %copy-start.1 = (s32[128,1]{0,1:T(1,128)S(1)}, s32[128,1]{0,1:T(1,128)}, u32[]{:S(2)}) copy-start(s32[128,1]{0,1:T(1,128)} %param.6) | copy-start | bytes 1540
  47.8 13.0 %copy-start.2 = (s32[128]{0:T(128)S(1)}, s32[128]{0:T(128)}, u32[]{:S(2)}) copy-start(s32[128]{0:T(128)} %param.5) | copy-start | bytes 1540
  56.2 8.8 %all-to-all-start = ((s32[4,1,40]{2,1,0:T(1,128)}), s32[4,1,40]{2,1,0:T(1,128)S(1)}, u32[]{:S(2)}, u32[]{:S(2)}) async-start(s32[4,1,40]{2,1,0:T(1,128)} %all_to_all.19), calls=%async_computation | async-start | bytes 4096 | tf_op jit(solution)/shard_map/all_to_all | solution.py:72
  93.2 1.4 copy-start
  95.8 35.3 %all-to-all-start.2 = ((bf16[4,40,4096]{2,1,0:T(8,128)(2,1)}), bf16[4,40,4096]{2,1,0:T(8,128)(2,1)S(1)}, u32[]{:S(2)}, u32[]{:S(2)}) async-start(bf16[4,40,4096]{2,1,0:T(8,128)(2,1)} %bitcast.8), calls=%async_computation.2 | async-start | bytes 2621440 | tf_op jit(solution)/shard_map/all_to_all | solution.py:81
Sparse Core Ops, SparseCore 0:
  54.1 29.3 all-gather.1
where the time goes:
time: 151 us; the launch traced here: 150 us
  other arithmetic  48.1 us (32%)
  waiting for transfers between devices  46.4 us (31%)
  local copies, waits for them, and re-layouts  23 us (15%)
  starting transfers between devices  14.1 us (9%)
  between operations  13.6 us (9%)
  matrix products  4.41 us (3%)
    another operation x3, other arithmetic  35 us
    all_to_all x1, waiting for transfers between devices, local(): lax.all_to_all(served.reshape(regions, capacity, width), 'region', split_...  25.1 us
    all_gather x1, waiting for transfers between devices, local(): piece = lax.all_gather(spectra, 'slab', axis=0, tiled=True)  17 us
    gather x1, local copies, waits for them, and re-layouts, local(): chosen = jnp.take(piece, jnp.clip(wanted, 0, piece.shape[0] - 1), axis=0)  9.32 us
    reduce_sum x1, other arithmetic, cross(): jnp.mean(left[..., 0, :] * right[..., 0, :] + left[..., 1, :] * right[......  5.77 us
    all_to_all x1, starting transfers between devices, local(): lax.all_to_all(records, 'slab', split_axis=0, concat_axis=1, tiled=True)  5.22 us
    all_to_all x1, starting transfers between devices, local(): lax.all_to_all(requests, 'region', split_axis=0, concat_axis=0, tiled=True)  4.59 us
    dot_general x1, matrix products, whitened(): spectrum = jnp.dot(tapered, dft_table(), preferred_element_type=jnp.float32)  4.41 us
  transfers between devices with their start and end apart: 4, of which 3 were waited for; matrix products, arithmetic and copies ran while one was open for 29% of the time, Pallas kernels for 0%

commit v1 on v0

--- a/solution.py
+++ b/solution.py
@@ -1,14 +1,204 @@
+import functools
 import math
 
 import jax
 import jax.numpy as jnp
+import numpy as np
 from jax import lax
+from jax.experimental import pallas as pl
+from jax.experimental.pallas import tpu as pltpu
 from jax.sharding import PartitionSpec as P
 
 NFFT = 2048
 BINS = 1024
 SEG = 2
 HALF = 4
+LANES = 128
+INDEX_ROWS = 8
+EXACT = 256
+AXES = ("region", "slab")
+
+
+def folded_tables():
+    half = NFFT // 2
+    sample = np.arange(half, dtype=np.int64)[:, None]
+    tables = []
+    for parity in (0, 1):
+        frequency = 2 * np.arange(half // 2, dtype=np.int64)[None, :] + parity
+        phase = (sample * frequency % NFFT) * (2.0 * math.pi / NFFT)
+        tables.append(np.concatenate([np.cos(phase), -np.sin(phase)], axis=1).astype(jnp.bfloat16))
+    return tables
+
+
+def interleaver():
+    order = np.zeros((2 * LANES, 2 * LANES), np.float32)
+    place = np.arange(LANES)
+    order[place, 2 * place] = 1.0
+    order[LANES + place, 2 * place + 1] = 1.0
+    return order.astype(jnp.bfloat16)
+
+
+def taper_row():
+    position = np.arange(NFFT, dtype=np.float64)
+    return (0.5 - 0.5 * np.cos(position * (2.0 * math.pi / NFFT))).astype(np.float32)[None, :]
+
+
+def shifted(values, step):
+    width = values.shape[1]
+    lane = lax.broadcasted_iota(jnp.int32, values.shape, 1)
+    moved = pltpu.roll(values, (-step) % width, 1)
+    return jnp.where((lane + step >= 0) & (lane + step < width), moved, 0.0)
+
+
+def spectra_kernel(x_ref, index_ref, taper_ref, even_ref, odd_ref, order_ref, out_ref):
+    slabs, count, _ = x_ref.shape
+    per_segment = slabs // SEG
+    half = NFFT // 2
+    sums, differences = [], []
+    for segment in range(SEG):
+        pieces = [x_ref[segment * per_segment + j].astype(jnp.float32) for j in range(per_segment)]
+        signal = jnp.concatenate(pieces, axis=1)
+        signal = signal - jnp.sum(signal, axis=1, keepdims=True) * (1.0 / NFFT)
+        signal = signal * taper_ref[...]
+        sums.append((signal[:, :half] + signal[:, half:]).astype(jnp.bfloat16))
+        differences.append((signal[:, :half] - signal[:, half:]).astype(jnp.bfloat16))
+    quarter = half // 2
+    even = jnp.dot(jnp.concatenate(sums, axis=0), even_ref[...], preferred_element_type=jnp.float32)
+    odd = jnp.dot(jnp.concatenate(differences, axis=0), odd_ref[...], preferred_element_type=jnp.float32)
+    size = []
+    for part in (even, odd):
+        real_part, imag_part = part[:, :quarter], part[:, quarter:]
+        size.append(jnp.sqrt(real_part * real_part + imag_part * imag_part + 1e-06))
+    level = (jnp.sum(size[0], axis=1, keepdims=True) + jnp.sum(size[1], axis=1, keepdims=True)) * (1.0 / BINS)
+    e = {step: shifted(size[0], step) if step else size[0] for step in (-2, -1, 0, 1, 2)}
+    o = {step: shifted(size[1], step) if step else size[1] for step in (-2, -1, 0, 1, 2)}
+    even_inner, odd_inner = e[-1] + e[0] + e[1], o[-1] + o[0] + o[1]
+    smooth_even = even_inner + e[-2] + e[2] + odd_inner + o[-2]
+    smooth_odd = odd_inner + o[-2] + o[2] + even_inner + e[2]
+    white = []
+    for part, smooth in ((even, smooth_even), (odd, smooth_odd)):
+        scale = 1.0 / (smooth * (1.0 / (2 * HALF + 1)) + level + 1e-06)
+        white.append([(part[:, :quarter] * scale).astype(jnp.bfloat16), (part[:, quarter:] * scale).astype(jnp.bfloat16)])
+    group = LANES // (2 * SEG)
+    lane_group = lax.broadcasted_iota(jnp.int32, (count, LANES), 1) // group
+    for j in range(BINS // (2 * LANES)):
+        lanes = slice(j * LANES, (j + 1) * LANES)
+        natural = []
+        for kind in (0, 1):
+            both = jnp.concatenate([white[0][kind][:, lanes], white[1][kind][:, lanes]], axis=1)
+            natural.append(jnp.dot(both, order_ref[...], preferred_element_type=jnp.float32))
+        for side in (0, 1):
+            sources = [
+                natural[kind][segment * count : (segment + 1) * count, side * LANES : (side + 1) * LANES]
+                for segment in range(SEG)
+                for kind in (0, 1)
+            ]
+            for q in range(2 * SEG):
+                block = None
+                for place, source in enumerate(sources):
+                    turn = (place - q) * group % LANES
+                    moved = pltpu.roll(source, turn, 1) if turn else source
+                    block = moved if block is None else jnp.where(lane_group == place, moved, block)
+                out_ref[(2 * j + side) * 2 * SEG + q, :count, :] = block.astype(jnp.bfloat16)
+    for dest in range(out_ref.shape[0]):
+        out_ref[dest, count:, :] = index_ref[...]
+
+
+def cross_kernel(regions, slabs, table_ref, out_ref, flipped_ref):
+    devices, rows, _ = table_ref.shape
+    count = rows - INDEX_ROWS
+    stations = slabs * count
+    bins = LANES // (2 * SEG)
+    per_step = 2
+    for region in range(regions):
+        block = table_ref[region * slabs : (region + 1) * slabs, :count, :].reshape(stations, LANES)
+        flipped_ref[region * LANES : (region + 1) * LANES, :] = block.T
+    station = lax.broadcasted_iota(jnp.int32, (stations, per_step * LANES), 0)
+
+    def step(i, _):
+        first_device = i * per_step
+
+        def named(row):
+            both = [table_ref[first_device + k, count : count + INDEX_ROWS, :].astype(jnp.float32)[row : row + 1] for k in range(per_step)]
+            return jnp.concatenate(both, axis=1).astype(jnp.int32)
+
+        first, second, target = named(0), named(1), named(2)
+        pick_first = (station == first).astype(jnp.float32).astype(jnp.bfloat16)
+        pick_second = (station == second).astype(jnp.float32).astype(jnp.bfloat16)
+        home = first_device // slabs
+        own = flipped_ref[pl.ds(pl.multiple_of(home * LANES, LANES), LANES), :]
+        a = jnp.dot(own, pick_first, preferred_element_type=jnp.float32)
+        b = None
+        for region in range(regions):
+            candidate = jnp.dot(flipped_ref[region * LANES : (region + 1) * LANES, :], pick_second, preferred_element_type=jnp.float32)
+            b = candidate if b is None else jnp.where(target == region, candidate, b)
+        real_sum, imag_sum = 0.0, 0.0
+        for segment in range(SEG):
+            at = 2 * segment * bins
+            ar, ai = a[at : at + bins], a[at + bins : at + 2 * bins]
+            br, bi = b[at : at + bins], b[at + bins : at + 2 * bins]
+            real_sum = real_sum + (ar * br + ai * bi)
+            imag_sum = imag_sum + (ar * bi - ai * br)
+        real_sum = (real_sum * (1.0 / SEG)).astype(jnp.bfloat16)
+        imag_sum = (imag_sum * (1.0 / SEG)).astype(jnp.bfloat16)
+        for k in range(per_step):
+            out_ref[first_device + k, :bins, :] = real_sum[:, k * LANES : (k + 1) * LANES]
+            out_ref[first_device + k, bins:, :] = imag_sum[:, k * LANES : (k + 1) * LANES]
+        return 0
+
+    lax.fori_loop(0, devices // per_step, step, 0, unroll=2)
+
+
+def place_kernel(in_ref, out_ref):
+    devices, rows, _ = in_ref.shape
+    bins = rows // 2
+    sources = LANES // bins
+    for kind in (0, 1):
+        for j in range(devices // sources):
+            block = in_ref[j * sources : (j + 1) * sources, kind * bins : (kind + 1) * bins, :]
+            at = kind * BINS + j * LANES
+            out_ref[:, at : at + LANES] = block.reshape(LANES, LANES).T
+
+
+def by_bins(records, first_station, second_region, second_station):
+    regions, slabs = lax.axis_size("region"), lax.axis_size("slab")
+    devices = regions * slabs
+    stations, samples = records.shape
+    count = stations // slabs
+    pair_count = first_station.shape[0]
+    named = jnp.stack([first_station, second_station, second_region.reshape(-1)])
+    index = jnp.pad(named, ((0, INDEX_ROWS - 3), (0, 0))).astype(jnp.bfloat16)
+    arrived = lax.all_to_all(records.reshape(slabs, count, samples), "slab", split_axis=0, concat_axis=0, tiled=True)
+    even, odd = folded_tables()
+    vmem = pl.BlockSpec(memory_space=pltpu.VMEM)
+    limit = pltpu.CompilerParams(vmem_limit_bytes=32 << 20)
+    sent = pl.pallas_call(
+        spectra_kernel,
+        out_shape=jax.ShapeDtypeStruct((devices, count + INDEX_ROWS, LANES), jnp.bfloat16),
+        in_specs=[vmem] * 6,
+        out_specs=vmem,
+        compiler_params=limit,
+        name="spectra",
+    )(arrived, index, jnp.asarray(taper_row()), jnp.asarray(even), jnp.asarray(odd), jnp.asarray(interleaver()))
+    table = lax.all_to_all(sent, AXES, split_axis=0, concat_axis=0, tiled=True)
+    partial = pl.pallas_call(
+        functools.partial(cross_kernel, regions, slabs),
+        out_shape=jax.ShapeDtypeStruct((devices, LANES // 2, pair_count), jnp.bfloat16),
+        in_specs=[vmem],
+        out_specs=vmem,
+        scratch_shapes=[pltpu.VMEM((regions * LANES, stations), jnp.bfloat16)],
+        compiler_params=limit,
+        name="cross",
+    )(table)
+    pieces = lax.all_to_all(partial, AXES, split_axis=0, concat_axis=0, tiled=True)
+    return pl.pallas_call(
+        place_kernel,
+        out_shape=jax.ShapeDtypeStruct((pair_count, 2 * BINS), jnp.bfloat16),
+        in_specs=[vmem],
+        out_specs=vmem,
+        compiler_params=limit,
+        name="place",
+    )(pieces)
 
 
 def dft_table():
@@ -43,16 +233,12 @@
 def cross(first_rows, second_rows):
     left = first_rows.astype(jnp.float32).reshape(first_rows.shape[:-1] + (SEG, 2, BINS))
     right = second_rows.astype(jnp.float32).reshape(second_rows.shape[:-1] + (SEG, 2, BINS))
-    real_sum = jnp.mean(
-        left[..., 0, :] * right[..., 0, :] + left[..., 1, :] * right[..., 1, :], axis=-2
-    )
-    imag_sum = jnp.mean(
-        left[..., 0, :] * right[..., 1, :] - left[..., 1, :] * right[..., 0, :], axis=-2
-    )
+    real_sum = jnp.mean(left[..., 0, :] * right[..., 0, :] + left[..., 1, :] * right[..., 1, :], axis=-2)
+    imag_sum = jnp.mean(left[..., 0, :] * right[..., 1, :] - left[..., 1, :] * right[..., 0, :], axis=-2)
     return jnp.concatenate([real_sum, imag_sum], axis=-1).astype(jnp.bfloat16)
 
 
-def local(records, first_station, second_region, second_station):
+def by_rows(records, first_station, second_region, second_station):
     regions = lax.axis_size("region")
     pair_count = first_station.shape[0]
     capacity = max(2, pair_count // regions + pair_count // 16)
@@ -63,36 +249,32 @@
     onehot = (target[:, None] == jnp.arange(regions, dtype=jnp.int32)[None, :]).astype(jnp.int32)
     ranking = jnp.sum((jnp.cumsum(onehot, axis=0) - onehot) * onehot, axis=1)
     slot_index = target * capacity + ranking
-    requests = (
-        jnp.zeros((regions * capacity,), jnp.int32)
-        .at[slot_index]
-        .set(second_station)
-        .reshape(regions, capacity)
-    )
+    requests = jnp.zeros((regions * capacity,), jnp.int32).at[slot_index].set(second_station).reshape(regions, capacity)
     incoming = lax.all_to_all(requests, "region", split_axis=0, concat_axis=0, tiled=True)
     wanted = jnp.concatenate([first_station, incoming.reshape(-1)])
-    initial = jnp.zeros((wanted.shape[0], width), jnp.bfloat16)
     piece = lax.all_gather(spectra, "slab", axis=0, tiled=True)
-    inside = (wanted >= 0) & (wanted < piece.shape[0])
-    chosen = jnp.take(piece, jnp.clip(wanted, 0, piece.shape[0] - 1), axis=0)
-    picked = jnp.where(inside[:, None], chosen, initial)
+    picked = jnp.take(piece, wanted, axis=0)
     first_rows = picked[:pair_count]
     served = picked[pair_count:]
     returned = lax.all_to_all(
         served.reshape(regions, capacity, width), "region", split_axis=0, concat_axis=0, tiled=True
     )
     second_rows = jnp.take(returned.reshape(regions * capacity, width), slot_index, axis=0)
-    stacks = cross(first_rows, second_rows)
-    return stacks
+    return cross(first_rows, second_rows)
+
+
+def local(records, first_station, second_region, second_station):
+    devices = lax.axis_size("region") * lax.axis_size("slab")
+    fits = 2 * SEG * BINS == LANES * devices and records.shape[0] <= EXACT and first_station.shape[0] == LANES
+    plan = by_bins if fits else by_rows
+    return plan(records, first_station, second_region, second_station)
 
 
 def solution(mesh):
     placed = (
-        P("region", "slab"),
-        P(("region", "slab")),
-        P(("region", "slab"), None),
-        P(("region", "slab")),
+        P(AXES[0], AXES[1]),
+        P(AXES),
+        P(AXES, None),
+        P(AXES),
     )
-    return jax.shard_map(
-        local, mesh=mesh, in_specs=placed, out_specs=P(("region", "slab"), None), check_vma=False
-    )
+    return jax.shard_map(local, mesh=mesh, in_specs=placed, out_specs=P(AXES, None), check_vma=False)

time: 151 us -> 56.5 us (0.37)
  other arithmetic: 48.1 us -> 1.34 us
  waiting for transfers between devices: 46.4 us -> 4.27 us
  blocking collectives: 0 us -> 34.3 us
  local copies, waits for them, and re-layouts: 23 us -> 4.78 us
  between operations: 13.6 us -> 0.02 us
  starting transfers between devices: 14.1 us -> 5.22 us
  Pallas kernels: 0 us -> 5.65 us
  matrix products: 4.41 us -> 0 us
    all_to_all x0 -> x2, blocking collectives: none -> 34.3 us  [the longest x1 18.1 us: by_bins(): lax.all_to_all(partial, AXES, split_axis=0, concat_axis=0, tiled=True)]
    another operation x4 -> x3, other arithmetic: 35.2 us -> 1.34 us  [by_bins(): jnp.stack([first_station, second_station, second_region.reshape(-1)])]
    all_to_all x3 -> x1, waiting for transfers between devices: 29.4 us -> 4.27 us  [by_bins(): lax.all_to_all(records.reshape(slabs, count, samples), 'slab', split_axis...]
    all_gather x1 -> x0, waiting for transfers between devices: 17 us -> none  [local(): piece = lax.all_gather(spectra, 'slab', axis=0, tiled=True)]
    gather x3 -> x0, local copies, waits for them, and re-layouts: 13.3 us -> none  [the longest x1 9.32 us: local(): chosen = jnp.take(piece, jnp.clip(wanted, 0, piece.shape[0] - 1), axis=0)]
    all_to_all x3 -> x1, starting transfers between devices: 14.1 us -> 5.22 us  [by_bins(): lax.all_to_all(records.reshape(slabs, count, samples), 'slab', split_axis...]
    reduce_sum x5 -> x0, other arithmetic: 6.36 us -> none  [the longest x1 5.77 us: cross(): jnp.mean(left[..., 0, :] * right[..., 0, :] + left[..., 1, :] * right[......]
    pallas_call x0 -> x3, Pallas kernels: none -> 5.65 us  [the longest x1 3.02 us: by_bins(): pl.pallas_call(functools.partial(cross_kernel, regions, slabs), out_shape...]
  transfers between devices with their start and end apart: 4 -> 1, of which waited for: 3 -> 1; matrix products, arithmetic and copies ran while one was open for 29% -> 2% of each run, Pallas kernels for 0% -> 0%
where the time goes in v1:
time: 56.5 us; the launch traced here: 55.5 us
  blocking collectives  34.3 us (61%)
  Pallas kernels  5.65 us (10%)
  starting transfers between devices  5.22 us (9%)
  local copies, waits for them, and re-layouts  4.78 us (8%)
  waiting for transfers between devices  4.27 us (8%)
  other arithmetic  1.34 us (2%)
    all_to_all x1, blocking collectives, by_bins(): lax.all_to_all(partial, AXES, split_axis=0, concat_axis=0, tiled=True)  18.1 us
    all_to_all x1, blocking collectives, by_bins(): table = lax.all_to_all(sent, AXES, split_axis=0, concat_axis=0, tiled=True)  16.1 us
    all_to_all x1, starting transfers between devices, by_bins(): lax.all_to_all(records.reshape(slabs, count, samples), 'slab', split_axis...  5.22 us
    unnamed x8, local copies, waits for them, and re-layouts  4.78 us
    all_to_all x1, waiting for transfers between devices, by_bins(): lax.all_to_all(records.reshape(slabs, count, samples), 'slab', split_axis...  4.27 us
    pallas_call x1, Pallas kernels, by_bins(): pl.pallas_call(functools.partial(cross_kernel, regions, slabs), out_shape...  3.02 us
    pallas_call x1, Pallas kernels, by_bins(): pl.pallas_call(spectra_kernel, out_shape=jax.ShapeDtypeStruct((devices, c...  1.65 us
    another operation x3, other arithmetic, by_bins(): jnp.stack([first_station, second_station, second_region.reshape(-1)])  1.34 us
  transfers between devices with their start and end apart: 1, of which 1 were waited for; matrix products, arithmetic and copies ran while one was open for 2% of the time, Pallas kernels for 0%

profile of v1, /device:TPU:1, one launch (start us, length us, event | category | flops | bytes accessed | tf_op | source)
XLA Modules:
  0.0 55.5 jit_solution(12669891172498710506)
XLA Ops:
  0.0 5.2 %all-to-all-start = ((bf16[8,32,512]{2,1,0:T(8,128)(2,1)}), bf16[8,32,512]{2,1,0:T(8,128)(2,1)S(1)}, u32[]{:S(2)}, u32[]{:S(2)}) async-start(bf16[8,32,512]{2,1,0:T(8,128)(2,1)} %bitcast.7), calls=%async_computation | async-start | bytes 524288 | tf_op jit(solution)/shard_map/all_to_all | solution.py:171
  5.2 0.7 %convert_bitcast_fusion.1 = (bf16[1,128]{1,0:T(2,128)(2,1)S(1)}, bf16[1,128]{1,0:T(2,128)(2,1)S(1)}) fusion(s32[128]{0:T(128)} %param.11, s32[128]{0:T(128)} %param.9), kind=kLoop, calls=%fused_computation.7 | loop fusion | flops 256 | bytes 1536 | tf_op jit(solution)/shard_map/stack | solution.py:169
  5.9 0.7 %convert_bitcast_fusion = bf16[1,128]{1,0:T(2,128)(2,1)S(1)} fusion(s32[128,1]{0,1:T(1,128)} %param.10), kind=kLoop, calls=%fused_computation.6 | loop fusion | flops 128 | bytes 768 | tf_op jit(solution)/shard_map/stack;reshape | solution.py:169
  6.6 4.3 %all-to-all-done.x_ref = bf16[8,32,512]{2,1,0:T(8,128)(2,1)S(1)} async-done(((bf16[8,32,512]{2,1,0:T(8,128)(2,1)}), bf16[8,32,512]{2,1,0:T(8,128)(2,1)S(1)}, u32[]{:S(2)}, u32[]{:S(2)}) %all-to-all-start) | async-done | bytes 262176 | tf_op jit(solution)/shard_map/all_to_all | solution.py:171
  10.8 0.0 copy-start
  10.8 1.6 %copy-done = bf16[1024,1024]{1,0:T(8,128)(2,1)S(1)} copy-done((bf16[1024,1024]{1,0:T(8,128)(2,1)S(1)}, bf16[1024,1024]{1,0:T(8,128)(2,1)}, u32[]{:S(2)}) %copy-start) | copy-done | bytes 2097176
  12.4 0.0 copy-start.1
  12.4 1.6 %copy-done.1 = bf16[1024,1024]{1,0:T(8,128)(2,1)S(1)} copy-done((bf16[1024,1024]{1,0:T(8,128)(2,1)S(1)}, bf16[1024,1024]{1,0:T(8,128)(2,1)}, u32[]{:S(2)}) %copy-start.1) | copy-done | bytes 2097176
  14.0 0.0 copy-start.2
  14.0 0.9 %copy-done.2 = bf16[256,256]{1,0:T(8,128)(2,1)S(1)} copy-done((bf16[256,256]{1,0:T(8,128)(2,1)S(1)}, bf16[256,256]{1,0:T(8,128)(2,1)}, u32[]{:S(2)}) %copy-start.2) | copy-done | bytes 131096
  14.9 0.0 copy-start.3
  14.9 0.7 %copy-done.3 = f32[1,2048]{1,0:T(1,128)S(1)} copy-done((f32[1,2048]{1,0:T(1,128)S(1)}, f32[1,2048]{1,0:T(1,128)}, u32[]{:S(2)}) %copy-start.3) | copy-done | bytes 8216
  15.6 1.7 %spectra.1 = bf16[32,40,128]{2,1,0:T(8,128)(2,1)S(1)} custom-call(bf16[8,32,512]{2,1,0:T(8,128)(2,1)S(1)} %all-to-all-done.x_ref, bf16[8,128]{1,0:T(8,128)(2,1)S(1)} %fusion.4.index_ref, f32[1,2048]{1,0:T(1,128)S(1)} %copy-done.3, bf16[1024,1024]{1,0:T(8,128)(2,1)S(1)} %copy-done.1, bf16[1024,1024]{1,0:T(8,128)(2,1)S(1)} %copy-done, ...), custom_call_target="tpu_custom_call" | custom-call | tf_op jit(solution)/shard_map/spectra/pallas_call | solution.py:175
  17.3 16.1 %all_to_all.15.table_ref = bf16[32,40,128]{2,1,0:T(8,128)(2,1)S(1)} all-to-all(bf16[32,40,128]{2,1,0:T(8,128)(2,1)S(1)} %spectra.1), channel_id=1, replica_groups=mesh['region'=4,'slab'=8] {'region','slab'}, dimensions={0} | all-to-all | bytes 655360 | tf_op jit(solution)/shard_map/all_to_all | solution.py:183
  33.4 3.0 %cross.1 = bf16[32,64,128]{2,1,0:T(8,128)(2,1)S(1)} custom-call(bf16[32,40,128]{2,1,0:T(8,128)(2,1)S(1)} %all_to_all.15.table_ref), custom_call_target="tpu_custom_call" | custom-call | tf_op jit(solution)/shard_map/cross/pallas_call | solution.py:184
  36.4 18.1 %all_to_all.16.in_ref = bf16[32,64,128]{2,1,0:T(8,128)(2,1)S(1)} all-to-all(bf16[32,64,128]{2,1,0:T(8,128)(2,1)S(1)} %cross.1), channel_id=1, replica_groups=mesh['region'=4,'slab'=8] {'region','slab'}, dimensions={0} | all-to-all | bytes 1048576 | tf_op jit(solution)/shard_map/all_to_all | solution.py:193
  54.6 1.0 %place.1 = bf16[128,2048]{1,0:T(8,128)(2,1)} custom-call(bf16[32,64,128]{2,1,0:T(8,128)(2,1)S(1)} %all_to_all.16.in_ref), custom_call_target="tpu_custom_call" | custom-call | tf_op jit(solution)/shard_map/place/pallas_call | solution.py:194
  (1 shorter events, 0.0 us)
Async XLA Ops:
  0.0 10.8 %all-to-all-start = ((bf16[8,32,512]{2,1,0:T(8,128)(2,1)}), bf16[8,32,512]{2,1,0:T(8,128)(2,1)S(1)}, u32[]{:S(2)}, u32[]{:S(2)}) async-start(bf16[8,32,512]{2,1,0:T(8,128)(2,1)} %bitcast.7), calls=%async_computation | async-start | bytes 524288 | tf_op jit(solution)/shard_map/all_to_all | solution.py:171
  10.8 1.6 %copy-start = (bf16[1024,1024]{1,0:T(8,128)(2,1)S(1)}, bf16[1024,1024]{1,0:T(8,128)(2,1)}, u32[]{:S(2)}) copy-start(bf16[1024,1024]{1,0:T(8,128)(2,1)} %constant.13.clone.odd_ref) | copy-start | bytes 6291460
  12.4 1.6 %copy-start.1 = (bf16[1024,1024]{1,0:T(8,128)(2,1)S(1)}, bf16[1024,1024]{1,0:T(8,128)(2,1)}, u32[]{:S(2)}) copy-start(bf16[1024,1024]{1,0:T(8,128)(2,1)} %constant.12.clone.even_ref) | copy-start | bytes 6291460
  14.0 0.9 %copy-start.2 = (bf16[256,256]{1,0:T(8,128)(2,1)S(1)}, bf16[256,256]{1,0:T(8,128)(2,1)}, u32[]{:S(2)}) copy-start(bf16[256,256]{1,0:T(8,128)(2,1)} %constant.14.clone.order_ref) | copy-start | bytes 393220
  14.9 0.7 %copy-start.3 = (f32[1,2048]{1,0:T(1,128)S(1)}, f32[1,2048]{1,0:T(1,128)}, u32[]{:S(2)}) copy-start(f32[1,2048]{1,0:T(1,128)} %constant.11.clone.taper_ref) | copy-start | bytes 24580

commit v2 on v1

v2 whole, which is shorter than its diff:
```python
import functools
import math

import jax
import jax.numpy as jnp
import numpy as np
from jax import lax
from jax.experimental import pallas as pl
from jax.experimental.pallas import tpu as pltpu
from jax.sharding import PartitionSpec as P

NFFT = 2048
BINS = 1024
SEG = 2
HALF = 4
LANES = 128
INDEX_ROWS = 8
RADIX = 16
SMALL_ROWS = 40
EXACT = 256
AXES = ("region", "slab")


def constant_rows():
    fine = np.arange(LANES, dtype=np.int64)
    twiddle = np.arange(RADIX // 2 + 1)[:, None] * fine[None, :] * (2.0 * math.pi / NFFT)
    position = np.arange(NFFT, dtype=np.float64).reshape(RADIX, LANES)
    taper = 0.5 - 0.5 * np.cos(position * (2.0 * math.pi / NFFT))
    mirrored = fine >= LANES // 2
    frequency = np.where(mirrored, LANES - 1 - (fine - LANES // 2), fine)
    phase = (fine[:, None] * frequency[None, :] % LANES) * (2.0 * math.pi / LANES)
    sign = np.where(mirrored, -1.0, 1.0)
    real_side = np.concatenate([np.cos(phase), np.sin(phase)], axis=0)
    imag_side = np.concatenate([-np.sin(phase) * sign, np.cos(phase) * sign], axis=0)
    matrix = np.concatenate([real_side, imag_side], axis=0).astype(jnp.bfloat16)
    small = np.concatenate([np.cos(twiddle), np.sin(twiddle), taper], axis=0)
    small = np.pad(small, ((0, SMALL_ROWS - small.shape[0]), (0, 0)))
    return np.concatenate([small, matrix.astype(np.float64)], axis=0).astype(np.float32)


def prepare_kernel(index_in_ref, rows_ref, index_ref, small_ref, matrix_ref):
    index_ref[...] = index_in_ref[...]
    small_ref[...] = rows_ref[:SMALL_ROWS, :]
    for side in (0, 1):
        at = SMALL_ROWS + side * 2 * LANES
        matrix_ref[:, side * LANES : (side + 1) * LANES] = rows_ref[at : at + 2 * LANES, :].astype(jnp.bfloat16)


def short_dft(pieces):
    half = RADIX // 2
    a = [pieces[j] + pieces[j + half] for j in range(half)]
    b = [pieces[j] - pieces[j + half] for j in range(half)]
    f = [a[j] + a[j + 4] for j in range(4)]
    g = [a[j] - a[j + 4] for j in range(4)]
    out = [None] * (half + 1)
    even, odd = f[0] + f[2], f[1] + f[3]
    root = math.sqrt(0.5)
    minus, plus = root * (g[1] - g[3]), root * (g[1] + g[3])
    out[0], out[8] = (even + odd, None), (even - odd, None)
    out[4] = (f[0] - f[2], f[3] - f[1])
    out[2] = (g[0] + minus, -(g[2] + plus))
    out[6] = (g[0] - minus, g[2] - plus)
    d = {j: b[j] - b[half - j] for j in (1, 2, 3)}
    e = {j: b[j] + b[half - j] for j in (1, 2, 3)}
    for k in (1, 3, 5, 7):
        real_part, imag_part = b[0], (-b[4] if k % 4 == 1 else b[4])
        for j in (1, 2, 3):
            real_part = real_part + d[j] * math.cos(math.pi * j * k / half)
            imag_part = imag_part - e[j] * math.sin(math.pi * j * k / half)
        out[k] = (real_part, imag_part)
    return out


def smoothed(size, lane):
    left = lane < LANES // 2
    inside = (lane > 0) & (lane < LANES - 1)

    def turned(values, by):
        return pltpu.roll(values, by, 1)

    line = {t: size[t] for t in range(1, 8)}
    line[0] = jnp.where(left, size[0], jnp.where(inside, turned(size[0], LANES // 2 - 1), 0.0))
    line[8] = jnp.where(left, turned(size[0], LANES // 2), size[0])
    for i in range(1, HALF + 1):
        line[8 + i] = turned(size[8 - i], LANES // 2)
        wrapped = jnp.where(left, turned(size[i], LANES // 2 + 1), turned(size[i], LANES // 2 - 1))
        line[-i] = jnp.where(inside, wrapped, 0.0)
    two = {t: line[t] + line[t + 1] for t in range(-HALF, 8 + HALF)}
    four = {t: two[t] + two[t + 2] for t in range(-HALF, 8 + HALF - 2)}
    nine = [four[t - 4] + four[t] + line[t + 4] for t in range(0, 9)]
    return [jnp.where(left, nine[0], nine[8])] + nine[1:8]


def spectra_kernel(x_ref, index_ref, small_ref, matrix_ref, out_ref):
    slabs, count, samples = x_ref.shape
    per_segment, per_piece = slabs // SEG, samples // LANES
    rows = SEG * count
    pieces = []
    for j in range(per_segment):
        both = jnp.concatenate([x_ref[segment * per_segment + j] for segment in range(SEG)], axis=0).astype(jnp.float32)
        pieces += [both[:, i * LANES : (i + 1) * LANES] for i in range(per_piece)]
    total = pieces[0]
    for piece in pieces[1:]:
        total = total + piece
    mean = jnp.sum(total, axis=1, keepdims=True) * (1.0 / NFFT)
    taper = 2 * (RADIX // 2 + 1)
    pieces = [(piece - mean) * small_ref[taper + n1 : taper + n1 + 1, :] for n1, piece in enumerate(pieces)]
    turned = []
    for k1, (real_part, imag_part) in enumerate(short_dft(pieces)):
        cosine = small_ref[k1 : k1 + 1, :]
        sine = small_ref[RADIX // 2 + 1 + k1 : RADIX // 2 + 2 + k1, :]
        if imag_part is None:
            both = [real_part * cosine, -real_part * sine]
        else:
            both = [real_part * cosine + imag_part * sine, imag_part * cosine - real_part * sine]
        turned.append(jnp.concatenate([part.astype(jnp.bfloat16) for part in both], axis=1))
    spectrum = jnp.dot(jnp.concatenate(turned, axis=0), matrix_ref[...], preferred_element_type=jnp.float32)
    lane = lax.broadcasted_iota(jnp.int32, (rows, LANES), 1)
    real_parts, imag_parts = (
        [spectrum[k1 * rows : (k1 + 1) * rows, side * LANES : (side + 1) * LANES] for k1 in range(RADIX // 2 + 1)]
        for side in (0, 1)
    )
    real_parts = [jnp.where(lane < LANES // 2, real_parts[0], real_parts[8])] + real_parts[1:8]
    imag_parts = [jnp.where(lane < LANES // 2, imag_parts[0], imag_parts[8])] + imag_parts[1:8]
    size = [jnp.sqrt(re * re + im * im + 1e-06) for re, im in zip(real_parts, imag_parts)]
    total = size[0]
    for part in size[1:]:
        total = total + part
    level = jnp.sum(total, axis=1, keepdims=True) * (1.0 / BINS) + 1e-06
    group = LANES // (2 * SEG)
    lane_group = lane[:count] // group
    for s, smooth in enumerate(smoothed(size, lane)):
        scale = 1.0 / (smooth * (1.0 / (2 * HALF + 1)) + level)
        white = [real_parts[s] * scale, imag_parts[s] * scale]
        sources = [part[segment * count : (segment + 1) * count] for segment in range(SEG) for part in white]
        for q in range(2 * SEG):
            block = None
            for place, source in enumerate(sources):
                turn = (place - q) * group % LANES
                moved = pltpu.roll(source, turn, 1) if turn else source
                block = moved if block is None else jnp.where(lane_group == place, moved, block)
            out_ref[2 * SEG * s + q, :count, :] = block.astype(jnp.bfloat16)
    for dest in range(out_ref.shape[0]):
        out_ref[dest, count:, :] = index_ref[...]


def cross_kernel(regions, slabs, table_ref, out_ref, flipped_ref):
    devices, rows, _ = table_ref.shape
    count = rows - INDEX_ROWS
    stations = slabs * count
    bins = LANES // (2 * SEG)
    per_step = 2
    for region in range(regions):
        block = table_ref[region * slabs : (region + 1) * slabs, :count, :].reshape(stations, LANES)
        flipped_ref[region * LANES : (region + 1) * LANES, :] = block.T
    station = lax.broadcasted_iota(jnp.int32, (stations, per_step * LANES), 0).astype(jnp.float32).astype(jnp.bfloat16)
    one, zero = jnp.ones((), jnp.bfloat16), jnp.zeros((), jnp.bfloat16)
    for first_device in range(0, devices, per_step):
        named = [table_ref[first_device + k, count:, :] for k in range(per_step)]
        named = jnp.concatenate(named, axis=1)
        first, second, target = named[0:1], named[1:2], named[2:3].astype(jnp.float32)
        home = first_device // slabs
        own = flipped_ref[home * LANES : (home + 1) * LANES, :]
        a = jnp.dot(own, jnp.where(station == first, one, zero), preferred_element_type=jnp.float32)
        pick_second = jnp.where(station == second, one, zero)
        b = None
        for region in range(regions):
            rows_of = flipped_ref[region * LANES : (region + 1) * LANES, :]
            candidate = jnp.dot(rows_of, pick_second, preferred_element_type=jnp.float32)
            b = candidate if b is None else jnp.where(target == region, candidate, b)
        real_sum, imag_sum = 0.0, 0.0
        for segment in range(SEG):
            at = 2 * segment * bins
            ar, ai = a[at : at + bins], a[at + bins : at + 2 * bins]
            br, bi = b[at : at + bins], b[at + bins : at + 2 * bins]
            real_sum = real_sum + (ar * br + ai * bi)
            imag_sum = imag_sum + (ar * bi - ai * br)
        real_sum = (real_sum * (1.0 / SEG)).astype(jnp.bfloat16)
        imag_sum = (imag_sum * (1.0 / SEG)).astype(jnp.bfloat16)
        for k in range(per_step):
            out_ref[first_device + k, :bins, :] = real_sum[:, k * LANES : (k + 1) * LANES]
            out_ref[first_device + k, bins:, :] = imag_sum[:, k * LANES : (k + 1) * LANES]


def place_kernel(in_ref, out_ref):
    devices, rows, _ = in_ref.shape
    bins = rows // 2
    fine = LANES // RADIX
    row = lax.broadcasted_iota(jnp.int32, (LANES, LANES), 0)
    lane = lax.broadcasted_iota(jnp.int32, (LANES, LANES), 1)
    slab, side = row // (2 * fine), row // fine % 2
    k1 = jnp.where(side == 0, slab, jnp.where(slab == 0, RADIX // 2, RADIX - slab))
    order = (lane == k1 + RADIX * (row % fine)).astype(jnp.float32).astype(jnp.bfloat16)
    per_slab = devices // (RADIX // 2)
    per_side = per_slab // 2
    for kind in (0, 1):
        for j in range(BINS // LANES):
            group, at = divmod(j * fine, bins)
            at += kind * bins
            picked = [in_ref[u * per_side + group, at : at + fine, :] for u in range(RADIX)]
            block = jnp.concatenate(picked, axis=0).T
            natural = jnp.dot(block, order, preferred_element_type=jnp.float32)
            place = kind * BINS + j * LANES
            out_ref[:, place : place + LANES] = natural.astype(jnp.bfloat16)


def by_bins(records, first_station, second_region, second_station):
    regions, slabs = lax.axis_size("region"), lax.axis_size("slab")
    devices = regions * slabs
    stations, samples = records.shape
    count = stations // slabs
    pair_count = first_station.shape[0]
    arrived = lax.all_to_all(records.reshape(slabs, count, samples), "slab", split_axis=0, concat_axis=0, tiled=True)
    named = jnp.stack([first_station, second_station, second_region.reshape(-1)])
    index = jnp.pad(named, ((0, INDEX_ROWS - 3), (0, 0))).astype(jnp.bfloat16)
    vmem = pl.BlockSpec(memory_space=pltpu.VMEM)
    limit = pltpu.CompilerParams(vmem_limit_bytes=12 << 20)
    prepared = pl.pallas_call(
        prepare_kernel,
        out_shape=[
            jax.ShapeDtypeStruct(index.shape, jnp.bfloat16),
            jax.ShapeDtypeStruct((SMALL_ROWS, LANES), jnp.float32),
            jax.ShapeDtypeStruct((2 * LANES, 2 * LANES), jnp.bfloat16),
        ],
        in_specs=[vmem] * 2,
        out_specs=[vmem] * 3,
        compiler_params=limit,
        cost_estimate=pl.CostEstimate(flops=NFFT * BINS, bytes_accessed=NFFT * BINS, transcendentals=0),
        name="prepare",
    )(index, jnp.asarray(constant_rows()))
    sent = pl.pallas_call(
        spectra_kernel,
        out_shape=jax.ShapeDtypeStruct((devices, count + INDEX_ROWS, LANES), jnp.bfloat16),
        in_specs=[vmem] * 4,
        out_specs=vmem,
        compiler_params=limit,
        name="spectra",
    )(arrived, *prepared)
    table = lax.all_to_all(sent, AXES, split_axis=0, concat_axis=0, tiled=True)
    partial = pl.pallas_call(
        functools.partial(cross_kernel, regions, slabs),
        out_shape=jax.ShapeDtypeStruct((devices, LANES // 2, pair_count), jnp.bfloat16),
        in_specs=[vmem],
        out_specs=vmem,
        scratch_shapes=[pltpu.VMEM((regions * LANES, stations), jnp.bfloat16)],
        compiler_params=limit,
        name="cross",
    )(table)
    pieces = lax.all_to_all(partial, AXES, split_axis=0, concat_axis=0, tiled=True)
    return pl.pallas_call(
        place_kernel,
        out_shape=jax.ShapeDtypeStruct((pair_count, 2 * BINS), jnp.bfloat16),
        in_specs=[vmem],
        out_specs=vmem,
        compiler_params=limit,
        name="place",
    )(pieces)


def dft_table():
    sample = jnp.arange(NFFT, dtype=jnp.int32)[:, None]
    frequency = jnp.arange(BINS, dtype=jnp.int32)[None, :]
    phase = (sample * frequency % NFFT).astype(jnp.float32) * (2.0 * math.pi / NFFT)
    return jnp.concatenate([jnp.cos(phase), -jnp.sin(phase)], axis=1).astype(jnp.bfloat16)


def whitened(traces):
    count = traces.shape[0]
    signal = traces.astype(jnp.float32).reshape(count * SEG, NFFT)
    signal = signal - jnp.mean(signal, axis=1, keepdims=True)
    position = jnp.arange(NFFT, dtype=jnp.int32).astype(jnp.float32)
    taper = 0.5 - 0.5 * jnp.cos(position * (2.0 * math.pi / NFFT))
    tapered = (signal * taper[None, :]).astype(jnp.bfloat16)
    spectrum = jnp.dot(tapered, dft_table(), preferred_element_type=jnp.float32)
    real_part = spectrum[:, :BINS]
    imag_part = spectrum[:, BINS:]
    amplitude = jnp.sqrt(real_part * real_part + imag_part * imag_part + 1e-06)
    padded = jnp.pad(amplitude, ((0, 0), (HALF, HALF)))
    smooth = jnp.zeros_like(amplitude)
    for offset in range(2 * HALF + 1):
        smooth = smooth + padded[:, offset : offset + BINS]
    smooth = smooth / (2 * HALF + 1)
    level = jnp.mean(amplitude, axis=1, keepdims=True)
    divisor = smooth + level + 1e-06
    white = spectrum / jnp.concatenate([divisor, divisor], axis=1)
    return white.astype(jnp.bfloat16).reshape(count, SEG * NFFT)


def cross(first_rows, second_rows):
    left = first_rows.astype(jnp.float32).reshape(first_rows.shape[:-1] + (SEG, 2, BINS))
    right = second_rows.astype(jnp.float32).reshape(second_rows.shape[:-1] + (SEG, 2, BINS))
    real_sum = jnp.mean(left[..., 0, :] * right[..., 0, :] + left[..., 1, :] * right[..., 1, :], axis=-2)
    imag_sum = jnp.mean(left[..., 0, :] * right[..., 1, :] - left[..., 1, :] * right[..., 0, :], axis=-2)
    return jnp.concatenate([real_sum, imag_sum], axis=-1).astype(jnp.bfloat16)


def by_rows(records, first_station, second_region, second_station):
    regions = lax.axis_size("region")
    pair_count = first_station.shape[0]
    capacity = max(2, pair_count // regions + pair_count // 16)
    arrived = lax.all_to_all(records, "slab", split_axis=0, concat_axis=1, tiled=True)
    spectra = whitened(arrived)
    width = spectra.shape[1]
    target = second_region[:, 0]
    onehot = (target[:, None] == jnp.arange(regions, dtype=jnp.int32)[None, :]).astype(jnp.int32)
    ranking = jnp.sum((jnp.cumsum(onehot, axis=0) - onehot) * onehot, axis=1)
    slot_index = target * capacity + ranking
    requests = jnp.zeros((regions * capacity,), jnp.int32).at[slot_index].set(second_station).reshape(regions, capacity)
    incoming = lax.all_to_all(requests, "region", split_axis=0, concat_axis=0, tiled=True)
    wanted = jnp.concatenate([first_station, incoming.reshape(-1)])
    piece = lax.all_gather(spectra, "slab", axis=0, tiled=True)
    picked = jnp.take(piece, wanted, axis=0)
    first_rows = picked[:pair_count]
    served = picked[pair_count:]
    returned = lax.all_to_all(
        served.reshape(regions, capacity, width), "region", split_axis=0, concat_axis=0, tiled=True
    )
    second_rows = jnp.take(returned.reshape(regions * capacity, width), slot_index, axis=0)
    return cross(first_rows, second_rows)


def local(records, first_station, second_region, second_station):
    devices = lax.axis_size("region") * lax.axis_size("slab")
    fits = 2 * SEG * BINS == LANES * devices and records.shape[0] <= EXACT and first_station.shape[0] == LANES
    plan = by_bins if fits else by_rows
    return plan(records, first_station, second_region, second_station)


def solution(mesh):
    placed = (
        P(AXES[0], AXES[1]),
        P(AXES),
        P(AXES, None),
        P(AXES),
    )
    return jax.shard_map(local, mesh=mesh, in_specs=placed, out_specs=P(AXES, None), check_vma=False)
```

time: 56.5 us -> 49.7 us (0.88)
  local copies, waits for them, and re-layouts: 4.78 us -> 0.65 us
  Pallas kernels: 5.65 us -> 3.68 us
  other arithmetic: 1.34 us -> 0.02 us
  waiting for transfers between devices: 4.27 us -> 4.89 us
    unnamed x8, local copies, waits for them, and re-layouts: 4.78 us -> 0.65 us
    pallas_call x1, Pallas kernels: 3.02 us -> 1.64 us  [by_bins(): pl.pallas_call(functools.partial(cross_kernel, regions, slabs), out_shape...]
    another operation x3, other arithmetic: 1.34 us -> 0.02 us  [by_bins(): jnp.stack([first_station, second_station, second_region.reshape(-1)])]
    pallas_call x1, Pallas kernels: 1.65 us -> 0.89 us  [by_bins(): pl.pallas_call(spectra_kernel, out_shape=jax.ShapeDtypeStruct((devices, c...]
    all_to_all x1, waiting for transfers between devices: 4.27 us -> 4.89 us  [by_bins(): lax.all_to_all(records.reshape(slabs, count, samples), 'slab', split_axis...]
  transfers between devices with their start and end apart: 1 -> 1, of which waited for: 1 -> 1; matrix products, arithmetic and copies ran while one was open for 2% -> 0% of each run, Pallas kernels for 0% -> 0%
where the time goes in v2:
time: 49.7 us; the launch traced here: 48.9 us
  blocking collectives  34.3 us (69%)
  starting transfers between devices  5.37 us (11%)
  waiting for transfers between devices  4.89 us (10%)
  Pallas kernels  3.68 us (7%)
  local copies, waits for them, and re-layouts  0.65 us (1%)
    all_to_all x1, blocking collectives, by_bins(): lax.all_to_all(partial, AXES, split_axis=0, concat_axis=0, tiled=True)  18.1 us
    all_to_all x1, blocking collectives, by_bins(): table = lax.all_to_all(sent, AXES, split_axis=0, concat_axis=0, tiled=True)  16.1 us
    all_to_all x1, starting transfers between devices, by_bins(): lax.all_to_all(records.reshape(slabs, count, samples), 'slab', split_axis...  5.37 us
    all_to_all x1, waiting for transfers between devices, by_bins(): lax.all_to_all(records.reshape(slabs, count, samples), 'slab', split_axis...  4.89 us
    pallas_call x1, Pallas kernels, by_bins(): pl.pallas_call(functools.partial(cross_kernel, regions, slabs), out_shape...  1.64 us
    pallas_call x1, Pallas kernels, by_bins(): pl.pallas_call(place_kernel, out_shape=jax.ShapeDtypeStruct((pair_count,...  1.13 us
  transfers between devices with their start and end apart: 1, of which 1 were waited for; matrix products, arithmetic and copies ran while one was open for 0% of the time, Pallas kernels for 0%

profile of v2, /device:TPU:1, one launch (start us, length us, event | category | flops | bytes accessed | tf_op | source)
XLA Modules:
  0.0 48.9 jit_solution(4036732010482482343)
XLA Ops:
  0.0 0.0 copy-start
  0.0 0.0 copy-start.1
  0.0 0.0 copy-start.2
  0.0 5.4 %all-to-all-start = ((bf16[8,32,512]{2,1,0:T(8,128)(2,1)}), bf16[8,32,512]{2,1,0:T(8,128)(2,1)S(1)}, u32[]{:S(2)}, u32[]{:S(2)}) async-start(bf16[8,32,512]{2,1,0:T(8,128)(2,1)} %bitcast.7), calls=%async_computation | async-start | bytes 524288 | tf_op jit(solution)/shard_map/all_to_all | solution.py:213
  5.4 0.0 copy-done.1
  5.4 0.0 copy-done.2
  5.4 0.0 copy-start.3
  5.4 0.6 %copy-done.3 = s32[128,1]{0,1:T(1,128)S(1)} copy-done((s32[128,1]{0,1:T(1,128)S(1)}, s32[128,1]{0,1:T(1,128)}, u32[]{:S(2)}) %copy-start.3) | copy-done | bytes 536
  6.1 0.0 copy-done
  6.1 4.9 %all-to-all-done.x_ref = bf16[8,32,512]{2,1,0:T(8,128)(2,1)S(1)} async-done(((bf16[8,32,512]{2,1,0:T(8,128)(2,1)}), bf16[8,32,512]{2,1,0:T(8,128)(2,1)S(1)}, u32[]{:S(2)}, u32[]{:S(2)}) %all-to-all-start) | async-done | bytes 262176 | tf_op jit(solution)/shard_map/all_to_all | solution.py:213
  11.0 0.9 %spectra.1 = bf16[32,40,128]{2,1,0:T(8,128)(2,1)S(1)} custom-call(bf16[8,32,512]{2,1,0:T(8,128)(2,1)S(1)} %all-to-all-done.x_ref, bf16[8,128]{1,0:T(8,128)(2,1)S(1)} %get-tuple-element.8.index_ref, f32[40,128]{1,0:T(8,128)S(1)} %get-tuple-element.9.small_ref, bf16[256,256]{1,0:T(8,128)(2,1)S(1)} %get-tuple-element.10.matrix_ref), custom_call_target="tpu_custom_call" | custom-call | tf_op jit(solution)/shard_map/spectra/pallas_call | solution.py:231
  11.9 16.1 %all_to_all.15.table_ref = bf16[32,40,128]{2,1,0:T(8,128)(2,1)S(1)} all-to-all(bf16[32,40,128]{2,1,0:T(8,128)(2,1)S(1)} %spectra.1), channel_id=1, replica_groups=mesh['region'=4,'slab'=8] {'region','slab'}, dimensions={0} | all-to-all | bytes 655360 | tf_op jit(solution)/shard_map/all_to_all | solution.py:239
  28.0 1.6 %cross.1 = bf16[32,64,128]{2,1,0:T(8,128)(2,1)S(1)} custom-call(bf16[32,40,128]{2,1,0:T(8,128)(2,1)S(1)} %all_to_all.15.table_ref), custom_call_target="tpu_custom_call" | custom-call | tf_op jit(solution)/shard_map/cross/pallas_call | solution.py:240
  29.7 18.1 %all_to_all.16.in_ref = bf16[32,64,128]{2,1,0:T(8,128)(2,1)S(1)} all-to-all(bf16[32,64,128]{2,1,0:T(8,128)(2,1)S(1)} %cross.1), channel_id=1, replica_groups=mesh['region'=4,'slab'=8] {'region','slab'}, dimensions={0} | all-to-all | bytes 1048576 | tf_op jit(solution)/shard_map/all_to_all | solution.py:249
  47.8 1.1 %place.1 = bf16[128,2048]{1,0:T(8,128)(2,1)} custom-call(bf16[32,64,128]{2,1,0:T(8,128)(2,1)S(1)} %all_to_all.16.in_ref), custom_call_target="tpu_custom_call" | custom-call | tf_op jit(solution)/shard_map/place/pallas_call | solution.py:250
  (4 shorter events, 0.0 us)
Async XLA Ops:
  0.0 6.1 %copy-start = (f32[552,128]{1,0:T(8,128)S(1)}, f32[552,128]{1,0:T(8,128)}, u32[]{:S(2)}) copy-start(f32[552,128]{1,0:T(8,128)} %constant.5.clone.rows_ref) | copy-start | bytes 847876
  0.0 5.4 %copy-start.1 = (s32[128]{0:T(128)S(1)}, s32[128]{0:T(128)}, u32[]{:S(2)}) copy-start(s32[128]{0:T(128)} %param.8) | copy-start | bytes 1540
  0.0 5.4 %copy-start.2 = (s32[128]{0:T(128)S(1)}, s32[128]{0:T(128)}, u32[]{:S(2)}) copy-start(s32[128]{0:T(128)} %param.6) | copy-start | bytes 1540
  0.0 11.0 %all-to-all-start = ((bf16[8,32,512]{2,1,0:T(8,128)(2,1)}), bf16[8,32,512]{2,1,0:T(8,128)(2,1)S(1)}, u32[]{:S(2)}, u32[]{:S(2)}) async-start(bf16[8,32,512]{2,1,0:T(8,128)(2,1)} %bitcast.7), calls=%async_computation | async-start | bytes 524288 | tf_op jit(solution)/shard_map/all_to_all | solution.py:213
  5.4 0.7 %copy-start.3 = (s32[128,1]{0,1:T(1,128)S(1)}, s32[128,1]{0,1:T(1,128)}, u32[]{:S(2)}) copy-start(s32[128,1]{0,1:T(1,128)} %param.7) | copy-start | bytes 1540

commit v3 on v2

--- a/solution.py
+++ b/solution.py
@@ -44,6 +44,22 @@
     for side in (0, 1):
         at = SMALL_ROWS + side * 2 * LANES
         matrix_ref[:, side * LANES : (side + 1) * LANES] = rows_ref[at : at + 2 * LANES, :].astype(jnp.bfloat16)
+
+
+def divide_kernel(records_ref, *refs):
+    parts = len(refs) - 1
+    targets, sem = refs[:-1], refs[-1]
+    rows = targets[0].shape[0]
+    own = lax.rem(lax.axis_index("slab"), parts)
+    copies = []
+    for k, target in enumerate(targets):
+        block = jnp.bitwise_xor(own, k)
+        source = records_ref.at[pl.ds(pl.multiple_of(block * rows, rows), rows), :]
+        copies.append(pltpu.make_async_copy(source, target, sem.at[k]))
+    for copy in copies:
+        copy.start()
+    for copy in copies:
+        copy.wait()
 
 
 def short_dft(pieces):
@@ -91,14 +107,20 @@
     return [jnp.where(left, nine[0], nine[8])] + nine[1:8]
 
 
-def spectra_kernel(x_ref, index_ref, small_ref, matrix_ref, out_ref):
-    slabs, count, samples = x_ref.shape
-    per_segment, per_piece = slabs // SEG, samples // LANES
-    rows = SEG * count
+def spectra_kernel(*refs):
+    parts = len(refs) - 4
+    index_ref, small_ref, matrix_ref, out_ref = refs[parts:]
+    rows, samples = refs[0].shape
+    count = rows // 2
+    own = lax.rem(lax.axis_index("slab"), parts)
+    blocks = [ref[...] for ref in refs[:parts]]
+    for bit in range(parts.bit_length() - 1):
+        swapped = jnp.bitwise_and(jnp.right_shift(own, bit), 1) == 1
+        blocks = [jnp.where(swapped, blocks[k ^ (1 << bit)], blocks[k]) for k in range(parts)]
     pieces = []
-    for j in range(per_segment):
-        both = jnp.concatenate([x_ref[segment * per_segment + j] for segment in range(SEG)], axis=0).astype(jnp.float32)
-        pieces += [both[:, i * LANES : (i + 1) * LANES] for i in range(per_piece)]
+    for block in blocks:
+        block = block.astype(jnp.float32)
+        pieces += [block[:, i * LANES : (i + 1) * LANES] for i in range(samples // LANES)]
     total = pieces[0]
     for piece in pieces[1:]:
         total = total + piece
@@ -127,19 +149,19 @@
     for part in size[1:]:
         total = total + part
     level = jnp.sum(total, axis=1, keepdims=True) * (1.0 / BINS) + 1e-06
-    group = LANES // (2 * SEG)
+    group = LANES // 4
     lane_group = lane[:count] // group
     for s, smooth in enumerate(smoothed(size, lane)):
         scale = 1.0 / (smooth * (1.0 / (2 * HALF + 1)) + level)
         white = [real_parts[s] * scale, imag_parts[s] * scale]
-        sources = [part[segment * count : (segment + 1) * count] for segment in range(SEG) for part in white]
-        for q in range(2 * SEG):
+        sources = [part[half * count : (half + 1) * count] for half in (0, 1) for part in white]
+        for q in range(4):
             block = None
             for place, source in enumerate(sources):
                 turn = (place - q) * group % LANES
                 moved = pltpu.roll(source, turn, 1) if turn else source
                 block = moved if block is None else jnp.where(lane_group == place, moved, block)
-            out_ref[2 * SEG * s + q, :count, :] = block.astype(jnp.bfloat16)
+            out_ref[4 * s + q, :count, :] = block.astype(jnp.bfloat16)
     for dest in range(out_ref.shape[0]):
         out_ref[dest, count:, :] = index_ref[...]
 
@@ -147,13 +169,22 @@
 def cross_kernel(regions, slabs, table_ref, out_ref, flipped_ref):
     devices, rows, _ = table_ref.shape
     count = rows - INDEX_ROWS
-    stations = slabs * count
-    bins = LANES // (2 * SEG)
+    parts = slabs // SEG
+    wide = parts * count
+    stations = 2 * wide
+    bins = LANES // 4
     per_step = 2
     for region in range(regions):
-        block = table_ref[region * slabs : (region + 1) * slabs, :count, :].reshape(stations, LANES)
-        flipped_ref[region * LANES : (region + 1) * LANES, :] = block.T
-    station = lax.broadcasted_iota(jnp.int32, (stations, per_step * LANES), 0).astype(jnp.float32).astype(jnp.bfloat16)
+        for segment in range(SEG):
+            first_source = region * slabs + segment * parts
+            block = table_ref[first_source : first_source + parts, :count, :].reshape(wide, LANES).T
+            at = region * LANES + segment * 2 * bins
+            for half in (0, 1):
+                flipped_ref[at : at + 2 * bins, half * wide : (half + 1) * wide] = block[half * 2 * bins : (half + 1) * 2 * bins]
+    column = lax.broadcasted_iota(jnp.int32, (stations, per_step * LANES), 0)
+    half, part = column // wide, column % wide // count
+    station = (part * 2 + half) * count + column % count
+    station = station.astype(jnp.float32).astype(jnp.bfloat16)
     one, zero = jnp.ones((), jnp.bfloat16), jnp.zeros((), jnp.bfloat16)
     for first_device in range(0, devices, per_step):
         named = [table_ref[first_device + k, count:, :] for k in range(per_step)]
@@ -208,13 +239,26 @@
     regions, slabs = lax.axis_size("region"), lax.axis_size("slab")
     devices = regions * slabs
     stations, samples = records.shape
-    count = stations // slabs
+    parts = slabs // SEG
+    rows = stations // parts
+    count = rows // 2
     pair_count = first_station.shape[0]
-    arrived = lax.all_to_all(records.reshape(slabs, count, samples), "slab", split_axis=0, concat_axis=0, tiled=True)
+    vmem = pl.BlockSpec(memory_space=pltpu.VMEM)
+    limit = pltpu.CompilerParams(vmem_limit_bytes=12 << 20)
+    divided = pl.pallas_call(
+        divide_kernel,
+        out_shape=[jax.ShapeDtypeStruct((rows, samples), records.dtype)] * parts,
+        in_specs=[pl.BlockSpec(memory_space=pl.ANY)],
+        out_specs=[vmem] * parts,
+        scratch_shapes=[pltpu.SemaphoreType.DMA((parts,))],
+        compiler_params=limit,
+        name="divide",
+    )(records)
+    arrived = [divided[0]] + [
+        lax.ppermute(divided[k], "slab", [(i, i ^ k) for i in range(slabs)]) for k in range(1, parts)
+    ]
     named = jnp.stack([first_station, second_station, second_region.reshape(-1)])
     index = jnp.pad(named, ((0, INDEX_ROWS - 3), (0, 0))).astype(jnp.bfloat16)
-    vmem = pl.BlockSpec(memory_space=pltpu.VMEM)
-    limit = pltpu.CompilerParams(vmem_limit_bytes=12 << 20)
     prepared = pl.pallas_call(
         prepare_kernel,
         out_shape=[
@@ -231,11 +275,11 @@
     sent = pl.pallas_call(
         spectra_kernel,
         out_shape=jax.ShapeDtypeStruct((devices, count + INDEX_ROWS, LANES), jnp.bfloat16),
-        in_specs=[vmem] * 4,
+        in_specs=[vmem] * (parts + 3),
         out_specs=vmem,
         compiler_params=limit,
         name="spectra",
-    )(arrived, *prepared)
+    )(*arrived, *prepared)
     table = lax.all_to_all(sent, AXES, split_axis=0, concat_axis=0, tiled=True)
     partial = pl.pallas_call(
         functools.partial(cross_kernel, regions, slabs),
@@ -320,8 +364,14 @@
 
 
 def local(records, first_station, second_region, second_station):
-    devices = lax.axis_size("region") * lax.axis_size("slab")
-    fits = 2 * SEG * BINS == LANES * devices and records.shape[0] <= EXACT and first_station.shape[0] == LANES
+    slabs = lax.axis_size("slab")
+    devices = lax.axis_size("region") * slabs
+    fits = (
+        devices * LANES == 4 * BINS
+        and records.shape == (EXACT, NFFT * SEG // slabs)
+        and slabs == 4 * SEG
+        and first_station.shape[0] == LANES
+    )
     plan = by_bins if fits else by_rows
     return plan(records, first_station, second_region, second_station)
 

time: 49.7 us -> 47.6 us (0.958)
  starting transfers between devices: 5.37 us -> 2.85 us
  waiting for transfers between devices: 4.89 us -> 2.38 us
  local copies, waits for them, and re-layouts: 0.65 us -> 2.51 us
  blocking collectives: 34.3 us -> 35 us
    all_to_all x1 -> x0, starting transfers between devices: 5.37 us -> none  [by_bins(): lax.all_to_all(records.reshape(slabs, count, samples), 'slab', split_axis...]
    all_to_all x1 -> x0, waiting for transfers between devices: 4.89 us -> none  [by_bins(): lax.all_to_all(records.reshape(slabs, count, samples), 'slab', split_axis...]
    ppermute x0 -> x3, starting transfers between devices: none -> 2.85 us  [by_bins(): lax.ppermute(divided[k], 'slab', [(i, i ^ k) for i in range(slabs)])]
    ppermute x0 -> x3, waiting for transfers between devices: none -> 2.38 us  [by_bins(): lax.ppermute(divided[k], 'slab', [(i, i ^ k) for i in range(slabs)])]
    unnamed x8 -> x10, local copies, waits for them, and re-layouts: 0.65 us -> 2.51 us
    all_to_all x1, blocking collectives: 16.1 us -> 16.9 us  [by_bins(): table = lax.all_to_all(sent, AXES, split_axis=0, concat_axis=0, tiled=True)]
  transfers between devices with their start and end apart: 1 -> 3, of which waited for: 1 -> 2; matrix products, arithmetic and copies ran while one was open for 0% -> 0% of each run, Pallas kernels for 0% -> 0%
where the time goes in v3:
time: 47.6 us; the launch traced here: 46.8 us
  blocking collectives  35 us (74%)
  Pallas kernels  4.04 us (8%)
  starting transfers between devices  2.85 us (6%)
  local copies, waits for them, and re-layouts  2.51 us (5%)
  waiting for transfers between devices  2.38 us (5%)
    all_to_all x1, blocking collectives, by_bins(): lax.all_to_all(partial, AXES, split_axis=0, concat_axis=0, tiled=True)  18.1 us
    all_to_all x1, blocking collectives, by_bins(): table = lax.all_to_all(sent, AXES, split_axis=0, concat_axis=0, tiled=True)  16.9 us
    ppermute x3, starting transfers between devices, by_bins(): lax.ppermute(divided[k], 'slab', [(i, i ^ k) for i in range(slabs)])  2.85 us
    unnamed x10, local copies, waits for them, and re-layouts  2.51 us
    ppermute x3, waiting for transfers between devices, by_bins(): lax.ppermute(divided[k], 'slab', [(i, i ^ k) for i in range(slabs)])  2.38 us
    pallas_call x1, Pallas kernels, by_bins(): pl.pallas_call(functools.partial(cross_kernel, regions, slabs), out_shape...  1.65 us
    pallas_call x1, Pallas kernels, by_bins(): pl.pallas_call(place_kernel, out_shape=jax.ShapeDtypeStruct((pair_count,...  1.13 us
  transfers between devices with their start and end apart: 3, of which 2 were waited for; matrix products, arithmetic and copies ran while one was open for 0% of the time, Pallas kernels for 0%

profile of v3, /device:TPU:1, one launch (start us, length us, event | category | flops | bytes accessed | tf_op | source)
XLA Modules:
  0.0 46.8 jit_solution(3422405541104623694)
XLA Ops:
  0.0 0.0 copy-start.1
  0.0 0.9 %copy-done.1 = bf16[256,512]{1,0:T(8,128)(2,1)S(1)} copy-done((bf16[256,512]{1,0:T(8,128)(2,1)S(1)}, bf16[256,512]{1,0:T(8,128)(2,1)}, u32[]{:S(2)}) %copy-start.1) | copy-done | bytes 262168
  1.0 0.3 divide.1
  1.3 0.1 collective-permute-start
  1.4 0.0 copy-start.4
  1.4 2.7 %collective-permute-start.1 = (bf16[64,512]{1,0:T(8,128)(2,1)S(1)}, bf16[64,512]{1,0:T(8,128)(2,1)S(1)}, u32[]{:S(2)}, u32[]{:S(2)}) collective-permute-start(bf16[64,512]{1,0:T(8,128)(2,1)S(1)} %get-tuple-element.14), channel_id=1, source_target_pairs={{0,2},{1,3},{2,0},{3,1},{4,6},{5,7},{6,4},{7,5},{8,10},{9,11},{10,... | collective-permute-start | bytes 196616 | tf_op jit(solution)/shard_map/ppermute | solution.py:258
  4.1 0.0 copy-start.2
  4.1 0.0 copy-start.3
  4.1 0.1 collective-permute-start.2
  4.2 0.0 copy-done.4
  4.2 0.6 %copy-done.2 = s32[128]{0:T(128)S(1)} copy-done((s32[128]{0:T(128)S(1)}, s32[128]{0:T(128)}, u32[]{:S(2)}) %copy-start.2) | copy-done | bytes 536
  4.8 0.0 copy-done.3
  4.8 0.0 copy-start
  4.8 0.9 %copy-done = f32[552,128]{1,0:T(8,128)S(1)} copy-done((f32[552,128]{1,0:T(8,128)S(1)}, f32[552,128]{1,0:T(8,128)}, u32[]{:S(2)}) %copy-start) | copy-done | bytes 282648
  5.8 0.0 collective-permute-done.refs_1_
  5.8 0.7 %collective-permute-done.1.refs_2_ = bf16[64,512]{1,0:T(8,128)(2,1)S(1)} collective-permute-done((bf16[64,512]{1,0:T(8,128)(2,1)S(1)}, bf16[64,512]{1,0:T(8,128)(2,1)S(1)}, u32[]{:S(2)}, u32[]{:S(2)}) %collective-permute-start.1) | collective-permute-done | bytes 65568 | tf_op jit(solution)/shard_map/ppermute | solution.py:258
  6.5 1.7 %collective-permute-done.2.refs_3_ = bf16[64,512]{1,0:T(8,128)(2,1)S(1)} collective-permute-done((bf16[64,512]{1,0:T(8,128)(2,1)S(1)}, bf16[64,512]{1,0:T(8,128)(2,1)S(1)}, u32[]{:S(2)}, u32[]{:S(2)}) %collective-permute-start.2) | collective-permute-done | bytes 65568 | tf_op jit(solution)/shard_map/ppermute | solution.py:258
  8.2 0.9 %spectra.1 = bf16[32,40,128]{2,1,0:T(8,128)(2,1)S(1)} custom-call(bf16[64,512]{1,0:T(8,128)(2,1)S(1)} %get-tuple-element.12.refs_0_, bf16[64,512]{1,0:T(8,128)(2,1)S(1)} %collective-permute-done.refs_1_, bf16[64,512]{1,0:T(8,128)(2,1)S(1)} %collective-permute-done.1.refs_2_, bf16[64,512]{1,0:T(8,128)(2,1)S(1)} %collective-permute-done.2.refs_3_, ...), custom_call_target="tpu_custom_call" | custom-call | tf_op jit(solution)/shard_map/spectra/pallas_call | solution.py:275
  9.1 16.9 %all_to_all.10.table_ref = bf16[32,40,128]{2,1,0:T(8,128)(2,1)S(1)} all-to-all(bf16[32,40,128]{2,1,0:T(8,128)(2,1)S(1)} %spectra.1), channel_id=1, replica_groups=mesh['region'=4,'slab'=8] {'region','slab'}, dimensions={0} | all-to-all | bytes 655360 | tf_op jit(solution)/shard_map/all_to_all | solution.py:283
  25.9 1.6 %cross.1 = bf16[32,64,128]{2,1,0:T(8,128)(2,1)S(1)} custom-call(bf16[32,40,128]{2,1,0:T(8,128)(2,1)S(1)} %all_to_all.10.table_ref), custom_call_target="tpu_custom_call" | custom-call | tf_op jit(solution)/shard_map/cross/pallas_call | solution.py:284
  27.6 18.1 %all_to_all.11.in_ref = bf16[32,64,128]{2,1,0:T(8,128)(2,1)S(1)} all-to-all(bf16[32,64,128]{2,1,0:T(8,128)(2,1)S(1)} %cross.1), channel_id=1, replica_groups=mesh['region'=4,'slab'=8] {'region','slab'}, dimensions={0} | all-to-all | bytes 1048576 | tf_op jit(solution)/shard_map/all_to_all | solution.py:293
  45.7 1.1 %place.1 = bf16[128,2048]{1,0:T(8,128)(2,1)} custom-call(bf16[32,64,128]{2,1,0:T(8,128)(2,1)S(1)} %all_to_all.11.in_ref), custom_call_target="tpu_custom_call" | custom-call | tf_op jit(solution)/shard_map/place/pallas_call | solution.py:294
  (4 shorter events, 0.0 us)
Async XLA Ops:
  0.0 0.9 %copy-start.1 = (bf16[256,512]{1,0:T(8,128)(2,1)S(1)}, bf16[256,512]{1,0:T(8,128)(2,1)}, u32[]{:S(2)}) copy-start(bf16[256,512]{1,0:T(8,128)(2,1)} %records_ref.1) | copy-start | bytes 786436
  1.3 4.5 %collective-permute-start = (bf16[64,512]{1,0:T(8,128)(2,1)S(1)}, bf16[64,512]{1,0:T(8,128)(2,1)S(1)}, u32[]{:S(2)}, u32[]{:S(2)}) collective-permute-start(bf16[64,512]{1,0:T(8,128)(2,1)S(1)} %get-tuple-element.13), channel_id=1, source_target_pairs={{0,1},{1,0},{2,3},{3,2},{4,5},{5,4},{6,7},{7,6},{8,9},{9,8},{10,11... | collective-permute-start | bytes 196616 | tf_op jit(solution)/shard_map/ppermute | solution.py:258
  1.4 2.7 %copy-start.4 = (s32[128,1]{0,1:T(1,128)S(1)}, s32[128,1]{0,1:T(1,128)}, u32[]{:S(2)}) copy-start(s32[128,1]{0,1:T(1,128)} %param.7) | copy-start | bytes 1540
  1.4 5.0 %collective-permute-start.1 = (bf16[64,512]{1,0:T(8,128)(2,1)S(1)}, bf16[64,512]{1,0:T(8,128)(2,1)S(1)}, u32[]{:S(2)}, u32[]{:S(2)}) collective-permute-start(bf16[64,512]{1,0:T(8,128)(2,1)S(1)} %get-tuple-element.14), channel_id=1, source_target_pairs={{0,2},{1,3},{2,0},{3,1},{4,6},{5,7},{6,4},{7,5},{8,10},{9,11},{10,... | collective-permute-start | bytes 196616 | tf_op jit(solution)/shard_map/ppermute | solution.py:258
  4.1 0.7 %copy-start.2 = (s32[128]{0:T(128)S(1)}, s32[128]{0:T(128)}, u32[]{:S(2)}) copy-start(s32[128]{0:T(128)} %param.8) | copy-start | bytes 1540
  4.1 0.7 %copy-start.3 = (s32[128]{0:T(128)S(1)}, s32[128]{0:T(128)}, u32[]{:S(2)}) copy-start(s32[128]{0:T(128)} %param.6) | copy-start | bytes 1540
  4.1 4.1 %collective-permute-start.2 = (bf16[64,512]{1,0:T(8,128)(2,1)S(1)}, bf16[64,512]{1,0:T(8,128)(2,1)S(1)}, u32[]{:S(2)}, u32[]{:S(2)}) collective-permute-start(bf16[64,512]{1,0:T(8,128)(2,1)S(1)} %get-tuple-element.15), channel_id=1, source_target_pairs={{0,3},{1,2},{2,1},{3,0},{4,7},{5,6},{6,5},{7,4},{8,11},{9,10},{10,... | collective-permute-start | bytes 196616 | tf_op jit(solution)/shard_map/ppermute | solution.py:258
  4.8 1.0 %copy-start = (f32[552,128]{1,0:T(8,128)S(1)}, f32[552,128]{1,0:T(8,128)}, u32[]{:S(2)}) copy-start(f32[552,128]{1,0:T(8,128)} %constant.5.clone.rows_ref) | copy-start | bytes 847876

commit v4 on v3

--- a/solution.py
+++ b/solution.py
@@ -14,11 +14,12 @@
 SEG = 2
 HALF = 4
 LANES = 128
-INDEX_ROWS = 8
+INDEX_ROWS = 4
 RADIX = 16
 SMALL_ROWS = 40
 EXACT = 256
 AXES = ("region", "slab")
+RANKS = ("slab", "region")
 
 
 def constant_rows():
@@ -46,20 +47,13 @@
         matrix_ref[:, side * LANES : (side + 1) * LANES] = rows_ref[at : at + 2 * LANES, :].astype(jnp.bfloat16)
 
 
-def divide_kernel(records_ref, *refs):
-    parts = len(refs) - 1
-    targets, sem = refs[:-1], refs[-1]
+def divide_kernel(records_ref, *targets):
+    parts = len(targets)
     rows = targets[0].shape[0]
     own = lax.rem(lax.axis_index("slab"), parts)
-    copies = []
     for k, target in enumerate(targets):
-        block = jnp.bitwise_xor(own, k)
-        source = records_ref.at[pl.ds(pl.multiple_of(block * rows, rows), rows), :]
-        copies.append(pltpu.make_async_copy(source, target, sem.at[k]))
-    for copy in copies:
-        copy.start()
-    for copy in copies:
-        copy.wait()
+        first = pl.multiple_of(jnp.bitwise_xor(own, k) * rows, rows)
+        target[...] = records_ref[pl.ds(first, rows), :]
 
 
 def short_dft(pieces):
@@ -161,13 +155,14 @@
                 turn = (place - q) * group % LANES
                 moved = pltpu.roll(source, turn, 1) if turn else source
                 block = moved if block is None else jnp.where(lane_group == place, moved, block)
-            out_ref[4 * s + q, :count, :] = block.astype(jnp.bfloat16)
-    for dest in range(out_ref.shape[0]):
-        out_ref[dest, count:, :] = index_ref[...]
+            at = (4 * s + q) * (count + INDEX_ROWS)
+            out_ref[at : at + count, :] = block.astype(jnp.bfloat16)
+            out_ref[at + count : at + count + INDEX_ROWS, :] = index_ref[...]
 
 
 def cross_kernel(regions, slabs, table_ref, out_ref, flipped_ref):
-    devices, rows, _ = table_ref.shape
+    devices = regions * slabs
+    rows = table_ref.shape[0] // devices
     count = rows - INDEX_ROWS
     parts = slabs // SEG
     wide = parts * count
@@ -176,8 +171,8 @@
     per_step = 2
     for region in range(regions):
         for segment in range(SEG):
-            first_source = region * slabs + segment * parts
-            block = table_ref[first_source : first_source + parts, :count, :].reshape(wide, LANES).T
+            sources = [((segment * parts + part) * regions + region) * rows for part in range(parts)]
+            block = jnp.concatenate([table_ref[at : at + count, :] for at in sources], axis=0).T
             at = region * LANES + segment * 2 * bins
             for half in (0, 1):
                 flipped_ref[at : at + 2 * bins, half * wide : (half + 1) * wide] = block[half * 2 * bins : (half + 1) * 2 * bins]
@@ -186,11 +181,12 @@
     station = (part * 2 + half) * count + column % count
     station = station.astype(jnp.float32).astype(jnp.bfloat16)
     one, zero = jnp.ones((), jnp.bfloat16), jnp.zeros((), jnp.bfloat16)
-    for first_device in range(0, devices, per_step):
-        named = [table_ref[first_device + k, count:, :] for k in range(per_step)]
+    for i in range(devices // per_step):
+        home, first_slab = i % regions, i // regions * per_step
+        owners = [(first_slab + k) * regions + home for k in range(per_step)]
+        named = [table_ref[owner * rows + count : (owner + 1) * rows, :] for owner in owners]
         named = jnp.concatenate(named, axis=1)
         first, second, target = named[0:1], named[1:2], named[2:3].astype(jnp.float32)
-        home = first_device // slabs
         own = flipped_ref[home * LANES : (home + 1) * LANES, :]
         a = jnp.dot(own, jnp.where(station == first, one, zero), preferred_element_type=jnp.float32)
         pick_second = jnp.where(station == second, one, zero)
@@ -208,9 +204,9 @@
             imag_sum = imag_sum + (ar * bi - ai * br)
         real_sum = (real_sum * (1.0 / SEG)).astype(jnp.bfloat16)
         imag_sum = (imag_sum * (1.0 / SEG)).astype(jnp.bfloat16)
-        for k in range(per_step):
-            out_ref[first_device + k, :bins, :] = real_sum[:, k * LANES : (k + 1) * LANES]
-            out_ref[first_device + k, bins:, :] = imag_sum[:, k * LANES : (k + 1) * LANES]
+        for k, owner in enumerate(owners):
+            out_ref[owner, :bins, :] = real_sum[:, k * LANES : (k + 1) * LANES]
+            out_ref[owner, bins:, :] = imag_sum[:, k * LANES : (k + 1) * LANES]
 
 
 def place_kernel(in_ref, out_ref):
@@ -248,15 +244,14 @@
     divided = pl.pallas_call(
         divide_kernel,
         out_shape=[jax.ShapeDtypeStruct((rows, samples), records.dtype)] * parts,
-        in_specs=[pl.BlockSpec(memory_space=pl.ANY)],
+        in_specs=[vmem],
         out_specs=[vmem] * parts,
-        scratch_shapes=[pltpu.SemaphoreType.DMA((parts,))],
         compiler_params=limit,
         name="divide",
     )(records)
-    arrived = [divided[0]] + [
-        lax.ppermute(divided[k], "slab", [(i, i ^ k) for i in range(slabs)]) for k in range(1, parts)
-    ]
+    arrived = list(divided)
+    for k in range(parts - 1, 0, -1):
+        arrived[k] = lax.ppermute(divided[k], "slab", [(i, i ^ k) for i in range(slabs)])
     named = jnp.stack([first_station, second_station, second_region.reshape(-1)])
     index = jnp.pad(named, ((0, INDEX_ROWS - 3), (0, 0))).astype(jnp.bfloat16)
     prepared = pl.pallas_call(
@@ -274,13 +269,14 @@
     )(index, jnp.asarray(constant_rows()))
     sent = pl.pallas_call(
         spectra_kernel,
-        out_shape=jax.ShapeDtypeStruct((devices, count + INDEX_ROWS, LANES), jnp.bfloat16),
+        out_shape=jax.ShapeDtypeStruct((devices * (count + INDEX_ROWS), LANES), jnp.bfloat16),
         in_specs=[vmem] * (parts + 3),
         out_specs=vmem,
         compiler_params=limit,
         name="spectra",
     )(*arrived, *prepared)
-    table = lax.all_to_all(sent, AXES, split_axis=0, concat_axis=0, tiled=True)
+    blocks = sent.reshape(devices, (count + INDEX_ROWS) // INDEX_ROWS, INDEX_ROWS, LANES)
+    table = lax.all_to_all(blocks, RANKS, split_axis=0, concat_axis=0, tiled=True).reshape(sent.shape)
     partial = pl.pallas_call(
         functools.partial(cross_kernel, regions, slabs),
         out_shape=jax.ShapeDtypeStruct((devices, LANES // 2, pair_count), jnp.bfloat16),
@@ -290,7 +286,7 @@
         compiler_params=limit,
         name="cross",
     )(table)
-    pieces = lax.all_to_all(partial, AXES, split_axis=0, concat_axis=0, tiled=True)
+    pieces = lax.all_to_all(partial, RANKS, split_axis=0, concat_axis=0, tiled=True)
     return pl.pallas_call(
         place_kernel,
         out_shape=jax.ShapeDtypeStruct((pair_count, 2 * BINS), jnp.bfloat16),

time: 47.6 us -> 46.1 us (0.968); the launches traced: 46.8 us -> 45.8 us
  blocking collectives: 35 us -> 34.3 us
    all_to_all x2, blocking collectives: 35 us -> 34.3 us  [the longest x1 17.8 us: by_bins(): lax.all_to_all(partial, RANKS, split_axis=0, concat_axis=0, tiled=True)]
where the time goes in v4:
time: 46.1 us; the launch traced here: 45.8 us
  blocking collectives  34.3 us (74%)
  Pallas kernels  3.74 us (8%)
  starting transfers between devices  2.85 us (6%)
  local copies, waits for them, and re-layouts  2.51 us (5%)
  waiting for transfers between devices  2.38 us (5%)
    all_to_all x1, blocking collectives, by_bins(): lax.all_to_all(partial, RANKS, split_axis=0, concat_axis=0, tiled=True)  17.8 us
    all_to_all x1, blocking collectives, by_bins(): lax.all_to_all(blocks, RANKS, split_axis=0, concat_axis=0, tiled=True)  16.5 us
    ppermute x3, starting transfers between devices, by_bins(): lax.ppermute(divided[k], 'slab', [(i, i ^ k) for i in range(slabs)])  2.85 us
    unnamed x10, local copies, waits for them, and re-layouts  2.51 us
    ppermute x3, waiting for transfers between devices, by_bins(): lax.ppermute(divided[k], 'slab', [(i, i ^ k) for i in range(slabs)])  2.38 us
    pallas_call x1, Pallas kernels, by_bins(): pl.pallas_call(functools.partial(cross_kernel, regions, slabs), out_shape...  1.67 us
    pallas_call x1, Pallas kernels, by_bins(): pl.pallas_call(place_kernel, out_shape=jax.ShapeDtypeStruct((pair_count,...  1.13 us
  transfers between devices with their start and end apart: 3, of which 2 were waited for; matrix products, arithmetic and copies ran while one was open for 0% of the time, Pallas kernels for 0%

profile of v4, /device:TPU:1, one launch (start us, length us, event | category | flops | bytes accessed | tf_op | source)
XLA Modules:
  0.0 45.8 jit_solution(743377408154000681)
XLA Ops:
  0.0 0.0 copy-start.1
  0.0 0.9 %copy-done.1 = bf16[256,512]{1,0:T(8,128)(2,1)S(1)} copy-done((bf16[256,512]{1,0:T(8,128)(2,1)S(1)}, bf16[256,512]{1,0:T(8,128)(2,1)}, u32[]{:S(2)}) %copy-start.1) | copy-done | bytes 262168
  1.0 0.1 collective-permute-start
  1.1 0.0 copy-start.4
  1.1 2.7 %collective-permute-start.1 = (bf16[64,512]{1,0:T(8,128)(2,1)S(1)}, bf16[64,512]{1,0:T(8,128)(2,1)S(1)}, u32[]{:S(2)}, u32[]{:S(2)}) collective-permute-start(bf16[64,512]{1,0:T(8,128)(2,1)S(1)} %get-tuple-element.14), channel_id=1, source_target_pairs={{0,2},{1,3},{2,0},{3,1},{4,6},{5,7},{6,4},{7,5},{8,10},{9,11},{10,... | collective-permute-start | bytes 196616 | tf_op jit(solution)/shard_map/ppermute | solution.py:254
  3.8 0.0 copy-start.2
  3.8 0.0 copy-start.3
  3.8 0.1 collective-permute-start.2
  3.8 0.0 copy-done.4
  3.8 0.6 %copy-done.2 = s32[128]{0:T(128)S(1)} copy-done((s32[128]{0:T(128)S(1)}, s32[128]{0:T(128)}, u32[]{:S(2)}) %copy-start.2) | copy-done | bytes 536
  4.4 0.0 copy-done.3
  4.5 0.0 copy-start
  4.5 0.9 %copy-done = f32[552,128]{1,0:T(8,128)S(1)} copy-done((f32[552,128]{1,0:T(8,128)S(1)}, f32[552,128]{1,0:T(8,128)}, u32[]{:S(2)}) %copy-start) | copy-done | bytes 282648
  5.4 0.0 collective-permute-done.refs_1_
  5.5 0.7 %collective-permute-done.1.refs_2_ = bf16[64,512]{1,0:T(8,128)(2,1)S(1)} collective-permute-done((bf16[64,512]{1,0:T(8,128)(2,1)S(1)}, bf16[64,512]{1,0:T(8,128)(2,1)S(1)}, u32[]{:S(2)}, u32[]{:S(2)}) %collective-permute-start.1) | collective-permute-done | bytes 65568 | tf_op jit(solution)/shard_map/ppermute | solution.py:254
  6.1 1.7 %collective-permute-done.2.refs_3_ = bf16[64,512]{1,0:T(8,128)(2,1)S(1)} collective-permute-done((bf16[64,512]{1,0:T(8,128)(2,1)S(1)}, bf16[64,512]{1,0:T(8,128)(2,1)S(1)}, u32[]{:S(2)}, u32[]{:S(2)}) %collective-permute-start.2) | collective-permute-done | bytes 65568 | tf_op jit(solution)/shard_map/ppermute | solution.py:254
  7.8 0.9 %spectra.1 = bf16[1152,128]{1,0:T(8,128)(2,1)S(1)} custom-call(bf16[64,512]{1,0:T(8,128)(2,1)S(1)} %get-tuple-element.12.refs_0_, bf16[64,512]{1,0:T(8,128)(2,1)S(1)} %collective-permute-done.refs_1_, bf16[64,512]{1,0:T(8,128)(2,1)S(1)} %collective-permute-done.1.refs_2_, bf16[64,512]{1,0:T(8,128)(2,1)S(1)} %collective-permute-done.2.refs_3_, ...), custom_call_target="tpu_custom_call" | custom-call | tf_op jit(solution)/shard_map/spectra/pallas_call | solution.py:270
  8.7 16.5 %all_to_all.10 = bf16[32,9,4,128]{3,2,1,0:T(4,128)(2,1)S(1)} all-to-all(bf16[32,9,4,128]{3,2,1,0:T(4,128)(2,1)S(1)} %bitcast.9), channel_id=1, replica_groups=mesh['region'=4,'slab'=8] {'slab','region'}, dimensions={0} | all-to-all | bytes 589824 | tf_op jit(solution)/shard_map/all_to_all | solution.py:279
  25.3 1.7 %cross.1 = bf16[32,64,128]{2,1,0:T(8,128)(2,1)S(1)} custom-call(bf16[1152,128]{1,0:T(8,128)(2,1)S(1)} %bitcast.8), custom_call_target="tpu_custom_call" | custom-call | tf_op jit(solution)/shard_map/cross/pallas_call | solution.py:280
  26.9 17.8 %all_to_all.11.in_ref = bf16[32,64,128]{2,1,0:T(8,128)(2,1)S(1)} all-to-all(bf16[32,64,128]{2,1,0:T(8,128)(2,1)S(1)} %cross.1), channel_id=1, replica_groups=mesh['region'=4,'slab'=8] {'slab','region'}, dimensions={0} | all-to-all | bytes 1048576 | tf_op jit(solution)/shard_map/all_to_all | solution.py:289
  44.7 1.1 %place.1 = bf16[128,2048]{1,0:T(8,128)(2,1)} custom-call(bf16[32,64,128]{2,1,0:T(8,128)(2,1)S(1)} %all_to_all.11.in_ref), custom_call_target="tpu_custom_call" | custom-call | tf_op jit(solution)/shard_map/place/pallas_call | solution.py:290
  (5 shorter events, 0.1 us)
Async XLA Ops:
  0.0 0.9 %copy-start.1 = (bf16[256,512]{1,0:T(8,128)(2,1)S(1)}, bf16[256,512]{1,0:T(8,128)(2,1)}, u32[]{:S(2)}) copy-start(bf16[256,512]{1,0:T(8,128)(2,1)} %records_ref.1) | copy-start | bytes 786436
  1.0 4.5 %collective-permute-start = (bf16[64,512]{1,0:T(8,128)(2,1)S(1)}, bf16[64,512]{1,0:T(8,128)(2,1)S(1)}, u32[]{:S(2)}, u32[]{:S(2)}) collective-permute-start(bf16[64,512]{1,0:T(8,128)(2,1)S(1)} %get-tuple-element.13), channel_id=1, source_target_pairs={{0,1},{1,0},{2,3},{3,2},{4,5},{5,4},{6,7},{7,6},{8,9},{9,8},{10,11... | collective-permute-start | bytes 196616 | tf_op jit(solution)/shard_map/ppermute | solution.py:254
  1.1 2.7 %copy-start.4 = (s32[128,1]{0,1:T(1,128)S(1)}, s32[128,1]{0,1:T(1,128)}, u32[]{:S(2)}) copy-start(s32[128,1]{0,1:T(1,128)} %param.7) | copy-start | bytes 1540
  1.1 5.0 %collective-permute-start.1 = (bf16[64,512]{1,0:T(8,128)(2,1)S(1)}, bf16[64,512]{1,0:T(8,128)(2,1)S(1)}, u32[]{:S(2)}, u32[]{:S(2)}) collective-permute-start(bf16[64,512]{1,0:T(8,128)(2,1)S(1)} %get-tuple-element.14), channel_id=1, source_target_pairs={{0,2},{1,3},{2,0},{3,1},{4,6},{5,7},{6,4},{7,5},{8,10},{9,11},{10,... | collective-permute-start | bytes 196616 | tf_op jit(solution)/shard_map/ppermute | solution.py:254
  3.8 0.7 %copy-start.2 = (s32[128]{0:T(128)S(1)}, s32[128]{0:T(128)}, u32[]{:S(2)}) copy-start(s32[128]{0:T(128)} %param.8) | copy-start | bytes 1540
  3.8 0.7 %copy-start.3 = (s32[128]{0:T(128)S(1)}, s32[128]{0:T(128)}, u32[]{:S(2)}) copy-start(s32[128]{0:T(128)} %param.6) | copy-start | bytes 1540
  3.8 4.1 %collective-permute-start.2 = (bf16[64,512]{1,0:T(8,128)(2,1)S(1)}, bf16[64,512]{1,0:T(8,128)(2,1)S(1)}, u32[]{:S(2)}, u32[]{:S(2)}) collective-permute-start(bf16[64,512]{1,0:T(8,128)(2,1)S(1)} %get-tuple-element.15), channel_id=1, source_target_pairs={{0,3},{1,2},{2,1},{3,0},{4,7},{5,6},{6,5},{7,4},{8,11},{9,10},{10,... | collective-permute-start | bytes 196616 | tf_op jit(solution)/shard_map/ppermute | solution.py:254
  4.5 1.0 %copy-start = (f32[552,128]{1,0:T(8,128)S(1)}, f32[552,128]{1,0:T(8,128)}, u32[]{:S(2)}) copy-start(f32[552,128]{1,0:T(8,128)} %constant.5.clone.rows_ref) | copy-start | bytes 847876

commit v5 on v4

--- a/solution.py
+++ b/solution.py
@@ -15,36 +15,53 @@
 HALF = 4
 LANES = 128
 INDEX_ROWS = 4
-RADIX = 16
-SMALL_ROWS = 40
+CLASSES = 4
+WIDTH = BINS // CLASSES
+COARSE, FINE = 16, 32
+TAPER_ROWS = 8
 EXACT = 256
 AXES = ("region", "slab")
 RANKS = ("slab", "region")
 
 
 def constant_rows():
-    fine = np.arange(LANES, dtype=np.int64)
-    twiddle = np.arange(RADIX // 2 + 1)[:, None] * fine[None, :] * (2.0 * math.pi / NFFT)
-    position = np.arange(NFFT, dtype=np.float64).reshape(RADIX, LANES)
-    taper = 0.5 - 0.5 * np.cos(position * (2.0 * math.pi / NFFT))
-    mirrored = fine >= LANES // 2
-    frequency = np.where(mirrored, LANES - 1 - (fine - LANES // 2), fine)
-    phase = (fine[:, None] * frequency[None, :] % LANES) * (2.0 * math.pi / LANES)
-    sign = np.where(mirrored, -1.0, 1.0)
-    real_side = np.concatenate([np.cos(phase), np.sin(phase)], axis=0)
-    imag_side = np.concatenate([-np.sin(phase) * sign, np.cos(phase) * sign], axis=0)
-    matrix = np.concatenate([real_side, imag_side], axis=0).astype(jnp.bfloat16)
-    small = np.concatenate([np.cos(twiddle), np.sin(twiddle), taper], axis=0)
-    small = np.pad(small, ((0, SMALL_ROWS - small.shape[0]), (0, 0)))
-    return np.concatenate([small, matrix.astype(np.float64)], axis=0).astype(np.float32)
-
-
-def prepare_kernel(index_in_ref, rows_ref, index_ref, small_ref, matrix_ref):
-    index_ref[...] = index_in_ref[...]
-    small_ref[...] = rows_ref[:SMALL_ROWS, :]
-    for side in (0, 1):
-        at = SMALL_ROWS + side * 2 * LANES
-        matrix_ref[:, side * LANES : (side + 1) * LANES] = rows_ref[at : at + 2 * LANES, :].astype(jnp.bfloat16)
+    rows = []
+    for pair in range(CLASSES // 2):
+        frequency = np.concatenate([CLASSES * np.arange(WIDTH, dtype=np.int64) + 2 * pair + side for side in (0, 1)])
+        for sample in (FINE * np.arange(COARSE, dtype=np.int64), np.arange(FINE, dtype=np.int64)):
+            phase = (sample[:, None] * frequency[None, :] % NFFT) * (2.0 * math.pi / NFFT)
+            rows += [np.cos(phase), np.sin(phase)]
+    angle = np.arange(NFFT, dtype=np.float32) * np.float32(2.0 * math.pi / NFFT)
+    cosine = np.cos(angle.astype(np.float64)).astype(np.float32)
+    taper = (np.float32(0.5) - np.float32(0.5) * cosine).reshape(CLASSES, -1)
+    rows.append(np.pad(taper, ((0, TAPER_ROWS - CLASSES), (0, 0))))
+    return np.concatenate(rows, axis=0).astype(np.float32)
+
+
+def prepare_kernel(named_ref, rows_ref, index_ref, taper_ref, table_ref):
+    row = lax.broadcasted_iota(jnp.int32, index_ref.shape, 0)
+    named = lax.rem(jnp.right_shift(named_ref[...], 8 * row), EXACT)
+    index_ref[...] = named.astype(jnp.float32).astype(jnp.bfloat16)
+    held = 2 * (COARSE + FINE)
+    taper_ref[...] = rows_ref[held * CLASSES // 2 :, :]
+    for pair in range(CLASSES // 2):
+        at = pair * held
+        fine_cos = rows_ref[at + 2 * COARSE : at + 2 * COARSE + FINE, :]
+        fine_sin = rows_ref[at + 2 * COARSE + FINE : at + held, :]
+
+        def block(i, _):
+            coarse_cos = rows_ref[pl.ds(at + i, 1), :]
+            coarse_sin = rows_ref[pl.ds(at + COARSE + i, 1), :]
+            cosine = (coarse_cos * fine_cos - coarse_sin * fine_sin).astype(jnp.bfloat16)
+            sine = (-coarse_sin * fine_cos - coarse_cos * fine_sin).astype(jnp.bfloat16)
+            for side in (0, 1):
+                first = (2 * pair + side) * FINE * COARSE + i * FINE
+                place = pl.ds(pl.multiple_of(first, FINE), FINE)
+                table_ref[place, :WIDTH] = cosine[:, side * WIDTH : (side + 1) * WIDTH]
+                table_ref[place, WIDTH:] = sine[:, side * WIDTH : (side + 1) * WIDTH]
+            return 0
+
+        lax.fori_loop(0, COARSE, block, 0, unroll=4)
 
 
 def divide_kernel(records_ref, *targets):
@@ -56,54 +73,22 @@
         target[...] = records_ref[pl.ds(first, rows), :]
 
 
-def short_dft(pieces):
-    half = RADIX // 2
-    a = [pieces[j] + pieces[j + half] for j in range(half)]
-    b = [pieces[j] - pieces[j + half] for j in range(half)]
-    f = [a[j] + a[j + 4] for j in range(4)]
-    g = [a[j] - a[j + 4] for j in range(4)]
-    out = [None] * (half + 1)
-    even, odd = f[0] + f[2], f[1] + f[3]
-    root = math.sqrt(0.5)
-    minus, plus = root * (g[1] - g[3]), root * (g[1] + g[3])
-    out[0], out[8] = (even + odd, None), (even - odd, None)
-    out[4] = (f[0] - f[2], f[3] - f[1])
-    out[2] = (g[0] + minus, -(g[2] + plus))
-    out[6] = (g[0] - minus, g[2] - plus)
-    d = {j: b[j] - b[half - j] for j in (1, 2, 3)}
-    e = {j: b[j] + b[half - j] for j in (1, 2, 3)}
-    for k in (1, 3, 5, 7):
-        real_part, imag_part = b[0], (-b[4] if k % 4 == 1 else b[4])
-        for j in (1, 2, 3):
-            real_part = real_part + d[j] * math.cos(math.pi * j * k / half)
-            imag_part = imag_part - e[j] * math.sin(math.pi * j * k / half)
-        out[k] = (real_part, imag_part)
-    return out
-
-
-def smoothed(size, lane):
-    left = lane < LANES // 2
-    inside = (lane > 0) & (lane < LANES - 1)
-
-    def turned(values, by):
-        return pltpu.roll(values, by, 1)
-
-    line = {t: size[t] for t in range(1, 8)}
-    line[0] = jnp.where(left, size[0], jnp.where(inside, turned(size[0], LANES // 2 - 1), 0.0))
-    line[8] = jnp.where(left, turned(size[0], LANES // 2), size[0])
-    for i in range(1, HALF + 1):
-        line[8 + i] = turned(size[8 - i], LANES // 2)
-        wrapped = jnp.where(left, turned(size[i], LANES // 2 + 1), turned(size[i], LANES // 2 - 1))
-        line[-i] = jnp.where(inside, wrapped, 0.0)
-    two = {t: line[t] + line[t + 1] for t in range(-HALF, 8 + HALF)}
-    four = {t: two[t] + two[t + 2] for t in range(-HALF, 8 + HALF - 2)}
-    nine = [four[t - 4] + four[t] + line[t + 4] for t in range(0, 9)]
-    return [jnp.where(left, nine[0], nine[8])] + nine[1:8]
+def shifted(values, step):
+    width = values.shape[1]
+    lane = lax.broadcasted_iota(jnp.int32, values.shape, 1)
+    moved = pltpu.roll(values, (-step) % width, 1)
+    return jnp.where((lane + step >= 0) & (lane + step < width), moved, 0.0)
+
+
+def two_terms(values):
+    coarse = values.astype(jnp.bfloat16)
+    fine = (values - coarse.astype(jnp.float32)).astype(jnp.bfloat16)
+    return jnp.concatenate([coarse, fine], axis=0)
 
 
 def spectra_kernel(*refs):
     parts = len(refs) - 4
-    index_ref, small_ref, matrix_ref, out_ref = refs[parts:]
+    index_ref, taper_ref, table_ref, out_ref = refs[parts:]
     rows, samples = refs[0].shape
     count = rows // 2
     own = lax.rem(lax.axis_index("slab"), parts)
@@ -111,53 +96,49 @@
     for bit in range(parts.bit_length() - 1):
         swapped = jnp.bitwise_and(jnp.right_shift(own, bit), 1) == 1
         blocks = [jnp.where(swapped, blocks[k ^ (1 << bit)], blocks[k]) for k in range(parts)]
-    pieces = []
-    for block in blocks:
-        block = block.astype(jnp.float32)
-        pieces += [block[:, i * LANES : (i + 1) * LANES] for i in range(samples // LANES)]
-    total = pieces[0]
-    for piece in pieces[1:]:
-        total = total + piece
-    mean = jnp.sum(total, axis=1, keepdims=True) * (1.0 / NFFT)
-    taper = 2 * (RADIX // 2 + 1)
-    pieces = [(piece - mean) * small_ref[taper + n1 : taper + n1 + 1, :] for n1, piece in enumerate(pieces)]
-    turned = []
-    for k1, (real_part, imag_part) in enumerate(short_dft(pieces)):
-        cosine = small_ref[k1 : k1 + 1, :]
-        sine = small_ref[RADIX // 2 + 1 + k1 : RADIX // 2 + 2 + k1, :]
-        if imag_part is None:
-            both = [real_part * cosine, -real_part * sine]
-        else:
-            both = [real_part * cosine + imag_part * sine, imag_part * cosine - real_part * sine]
-        turned.append(jnp.concatenate([part.astype(jnp.bfloat16) for part in both], axis=1))
-    spectrum = jnp.dot(jnp.concatenate(turned, axis=0), matrix_ref[...], preferred_element_type=jnp.float32)
-    lane = lax.broadcasted_iota(jnp.int32, (rows, LANES), 1)
-    real_parts, imag_parts = (
-        [spectrum[k1 * rows : (k1 + 1) * rows, side * LANES : (side + 1) * LANES] for k1 in range(RADIX // 2 + 1)]
-        for side in (0, 1)
-    )
-    real_parts = [jnp.where(lane < LANES // 2, real_parts[0], real_parts[8])] + real_parts[1:8]
-    imag_parts = [jnp.where(lane < LANES // 2, imag_parts[0], imag_parts[8])] + imag_parts[1:8]
-    size = [jnp.sqrt(re * re + im * im + 1e-06) for re, im in zip(real_parts, imag_parts)]
-    total = size[0]
-    for part in size[1:]:
-        total = total + part
-    level = jnp.sum(total, axis=1, keepdims=True) * (1.0 / BINS) + 1e-06
+    blocks = [block.astype(jnp.float32) for block in blocks]
+    mean = jnp.sum((blocks[0] + blocks[1]) + (blocks[2] + blocks[3]), axis=1, keepdims=True) * (1.0 / NFFT)
+    blocks = [((block - mean) * taper_ref[j : j + 1, :]).astype(jnp.bfloat16) for j, block in enumerate(blocks)]
+    blocks = [block.astype(jnp.float32) for block in blocks]
+
+    def transformed(values, r):
+        table = table_ref[r * samples : (r + 1) * samples, :]
+        both = jnp.dot(two_terms(values), table, preferred_element_type=jnp.float32)
+        both = both[: values.shape[0]] + both[values.shape[0] :]
+        return both[:, :WIDTH], both[:, WIDTH:]
+
+    added, taken = ([blocks[j] + sign * blocks[j + 2] for j in (0, 1)] for sign in (1.0, -1.0))
+    spectrum = [None] * CLASSES
+    spectrum[0] = transformed(added[0] + added[1], 0)
+    spectrum[2] = transformed(added[0] - added[1], 2)
+    for r, sign in ((1, 1.0), (3, -1.0)):
+        with_cos, with_sin = transformed(jnp.concatenate(taken, axis=0), r)
+        spectrum[r] = (with_cos[:rows] + sign * with_sin[rows:], with_sin[:rows] - sign * with_cos[rows:])
+    size = [jnp.sqrt(re * re + im * im + 1e-06) for re, im in spectrum]
+    every = (size[0] + size[1]) + (size[2] + size[3])
+    level = jnp.sum(every, axis=1, keepdims=True) * (1.0 / BINS) + 1e-06
+    before, after = ([shifted(part, step) for part in size] for step in (-1, 1))
     group = LANES // 4
-    lane_group = lane[:count] // group
-    for s, smooth in enumerate(smoothed(size, lane)):
+    lane_group = lax.broadcasted_iota(jnp.int32, (count, LANES), 1) // group
+    for r in range(CLASSES):
+        smooth = every
+        for part in before[r:] + after[: r + 1]:
+            smooth = smooth + part
         scale = 1.0 / (smooth * (1.0 / (2 * HALF + 1)) + level)
-        white = [real_parts[s] * scale, imag_parts[s] * scale]
-        sources = [part[half * count : (half + 1) * count] for half in (0, 1) for part in white]
-        for q in range(4):
-            block = None
-            for place, source in enumerate(sources):
-                turn = (place - q) * group % LANES
-                moved = pltpu.roll(source, turn, 1) if turn else source
-                block = moved if block is None else jnp.where(lane_group == place, moved, block)
-            at = (4 * s + q) * (count + INDEX_ROWS)
-            out_ref[at : at + count, :] = block.astype(jnp.bfloat16)
-            out_ref[at + count : at + count + INDEX_ROWS, :] = index_ref[...]
+        white = [(part * scale).astype(jnp.bfloat16) for part in spectrum[r]]
+        for s in range(WIDTH // LANES):
+            sources = [
+                part[side * count : (side + 1) * count, s * LANES : (s + 1) * LANES] for side in (0, 1) for part in white
+            ]
+            for q in range(4):
+                block = None
+                for place, source in enumerate(sources):
+                    turn = (place - q) * group % LANES
+                    moved = pltpu.roll(source, turn, 1) if turn else source
+                    block = moved if block is None else jnp.where(lane_group == place, moved, block)
+                at = (r * WIDTH // group + 4 * s + q) * (count + INDEX_ROWS)
+                out_ref[at : at + count, :] = block
+                out_ref[at + count : at + count + INDEX_ROWS, :] = index_ref[...]
 
 
 def cross_kernel(regions, slabs, table_ref, out_ref, flipped_ref):
@@ -212,20 +193,13 @@
 def place_kernel(in_ref, out_ref):
     devices, rows, _ = in_ref.shape
     bins = rows // 2
-    fine = LANES // RADIX
     row = lax.broadcasted_iota(jnp.int32, (LANES, LANES), 0)
     lane = lax.broadcasted_iota(jnp.int32, (LANES, LANES), 1)
-    slab, side = row // (2 * fine), row // fine % 2
-    k1 = jnp.where(side == 0, slab, jnp.where(slab == 0, RADIX // 2, RADIX - slab))
-    order = (lane == k1 + RADIX * (row % fine)).astype(jnp.float32).astype(jnp.bfloat16)
-    per_slab = devices // (RADIX // 2)
-    per_side = per_slab // 2
+    order = (lane == CLASSES * (row % bins) + row // bins).astype(jnp.float32).astype(jnp.bfloat16)
     for kind in (0, 1):
-        for j in range(BINS // LANES):
-            group, at = divmod(j * fine, bins)
-            at += kind * bins
-            picked = [in_ref[u * per_side + group, at : at + fine, :] for u in range(RADIX)]
-            block = jnp.concatenate(picked, axis=0).T
+        for j in range(devices // CLASSES):
+            sources = range(j, devices, devices // CLASSES)
+            block = jnp.concatenate([in_ref[u, kind * bins : (kind + 1) * bins, :] for u in sources], axis=0).T
             natural = jnp.dot(block, order, preferred_element_type=jnp.float32)
             place = kind * BINS + j * LANES
             out_ref[:, place : place + LANES] = natural.astype(jnp.bfloat16)
@@ -252,21 +226,20 @@
     arrived = list(divided)
     for k in range(parts - 1, 0, -1):
         arrived[k] = lax.ppermute(divided[k], "slab", [(i, i ^ k) for i in range(slabs)])
-    named = jnp.stack([first_station, second_station, second_region.reshape(-1)])
-    index = jnp.pad(named, ((0, INDEX_ROWS - 3), (0, 0))).astype(jnp.bfloat16)
+    named = first_station + EXACT * second_station + EXACT * EXACT * second_region.reshape(-1)
     prepared = pl.pallas_call(
         prepare_kernel,
         out_shape=[
-            jax.ShapeDtypeStruct(index.shape, jnp.bfloat16),
-            jax.ShapeDtypeStruct((SMALL_ROWS, LANES), jnp.float32),
-            jax.ShapeDtypeStruct((2 * LANES, 2 * LANES), jnp.bfloat16),
+            jax.ShapeDtypeStruct((INDEX_ROWS, pair_count), jnp.bfloat16),
+            jax.ShapeDtypeStruct((TAPER_ROWS, samples), jnp.float32),
+            jax.ShapeDtypeStruct((CLASSES * samples, 2 * WIDTH), jnp.bfloat16),
         ],
         in_specs=[vmem] * 2,
         out_specs=[vmem] * 3,
         compiler_params=limit,
         cost_estimate=pl.CostEstimate(flops=NFFT * BINS, bytes_accessed=NFFT * BINS, transcendentals=0),
         name="prepare",
-    )(index, jnp.asarray(constant_rows()))
+    )(named.reshape(1, -1), jnp.asarray(constant_rows()))
     sent = pl.pallas_call(
         spectra_kernel,
         out_shape=jax.ShapeDtypeStruct((devices * (count + INDEX_ROWS), LANES), jnp.bfloat16),

time: 46.1 us -> 46.4 us (level)
  Pallas kernels: 3.74 us -> 4.84 us
  waiting for transfers between devices: 2.38 us -> 1.49 us
  other arithmetic: 0.02 us -> 0.69 us
  local copies, waits for them, and re-layouts: 2.51 us -> 1.95 us
    ppermute x3, waiting for transfers between devices: 2.38 us -> 1.49 us  [by_bins(): lax.ppermute(divided[k], 'slab', [(i, i ^ k) for i in range(slabs)])]
    pallas_call x1, Pallas kernels: 0.02 us -> 0.8 us  [by_bins(): pl.pallas_call(prepare_kernel, out_shape=[jax.ShapeDtypeStruct((INDEX_ROW...]
    reshape x0 -> x1, other arithmetic: none -> 0.69 us  [by_bins(): named.reshape(1, -1)]
    unnamed x10 -> x4, local copies, waits for them, and re-layouts: 2.51 us -> 1.95 us
  transfers between devices with their start and end apart: 3 -> 3, of which waited for: 2 -> 1; matrix products, arithmetic and copies ran while one was open for 0% -> 1% of each run, Pallas kernels for 0% -> 2%
where the time goes in v5:
time: 46.4 us; the launch traced here: 46.2 us
  blocking collectives  34.3 us (74%)
  Pallas kernels  4.84 us (10%)
  starting transfers between devices  2.84 us (6%)
  local copies, waits for them, and re-layouts  1.95 us (4%)
  waiting for transfers between devices  1.49 us (3%)
  other arithmetic  0.69 us (1%)
    all_to_all x1, blocking collectives, by_bins(): lax.all_to_all(partial, RANKS, split_axis=0, concat_axis=0, tiled=True)  17.7 us
    all_to_all x1, blocking collectives, by_bins(): lax.all_to_all(blocks, RANKS, split_axis=0, concat_axis=0, tiled=True)  16.6 us
    ppermute x3, starting transfers between devices, by_bins(): lax.ppermute(divided[k], 'slab', [(i, i ^ k) for i in range(slabs)])  2.84 us
    unnamed x4, local copies, waits for them, and re-layouts  1.95 us
    pallas_call x1, Pallas kernels, by_bins(): pl.pallas_call(functools.partial(cross_kernel, regions, slabs), out_shape...  1.68 us
    ppermute x3, waiting for transfers between devices, by_bins(): lax.ppermute(divided[k], 'slab', [(i, i ^ k) for i in range(slabs)])  1.49 us
    pallas_call x1, Pallas kernels, by_bins(): pl.pallas_call(spectra_kernel, out_shape=jax.ShapeDtypeStruct((devices *...  1.22 us
    pallas_call x1, Pallas kernels, by_bins(): pl.pallas_call(place_kernel, out_shape=jax.ShapeDtypeStruct((pair_count,...  1.13 us
  transfers between devices with their start and end apart: 3, of which 1 were waited for; matrix products, arithmetic and copies ran while one was open for 1% of the time, Pallas kernels for 2%

profile of v5, /device:TPU:1, one launch (start us, length us, event | category | flops | bytes accessed | tf_op | source)
XLA Modules:
  0.0 46.2 jit_solution(9013575903523931336)
XLA Ops:
  0.0 0.0 copy-start.1
  0.0 0.9 %copy-done.1 = bf16[256,512]{1,0:T(8,128)(2,1)S(1)} copy-done((bf16[256,512]{1,0:T(8,128)(2,1)S(1)}, bf16[256,512]{1,0:T(8,128)(2,1)}, u32[]{:S(2)}) %copy-start.1) | copy-done | bytes 262168
  1.0 0.1 collective-permute-start
  1.1 2.7 %collective-permute-start.1 = (bf16[64,512]{1,0:T(8,128)(2,1)S(1)}, bf16[64,512]{1,0:T(8,128)(2,1)S(1)}, u32[]{:S(2)}, u32[]{:S(2)}) collective-permute-start(bf16[64,512]{1,0:T(8,128)(2,1)S(1)} %get-tuple-element.14), channel_id=1, source_target_pairs={{0,2},{1,3},{2,0},{3,1},{4,6},{5,7},{6,4},{7,5},{8,10},{9,11},{10,... | collective-permute-start | bytes 196616 | tf_op jit(solution)/shard_map/ppermute | solution.py:228
  3.8 0.0 collective-permute-start.2
  3.8 0.7 %fusion.named_ref = s32[1,128]{1,0:T(1,128)S(1)} fusion(s32[128,1]{0,1:T(1,128)} %param.7, s32[128]{0:T(128)} %param.6, s32[128]{0:T(128)} %param.8), kind=kLoop, calls=%fused_computation.1 | loop fusion | flops 512 | bytes 2048 | tf_op jit(solution)/shard_map/reshape | solution.py:242
  4.5 0.0 copy-start
  4.5 1.0 %copy-done = f32[200,512]{1,0:T(8,128)S(1)} copy-done((f32[200,512]{1,0:T(8,128)S(1)}, f32[200,512]{1,0:T(8,128)}, u32[]{:S(2)}) %copy-start) | copy-done | bytes 409624
  5.5 0.8 %prepare.1 = (bf16[4,128]{1,0:T(4,128)(2,1)S(1)}, f32[8,512]{1,0:T(8,128)S(1)}, bf16[2048,512]{1,0:T(8,128)(2,1)S(1)}) custom-call(s32[1,128]{1,0:T(1,128)S(1)} %fusion.named_ref, f32[200,512]{1,0:T(8,128)S(1)} %copy-done), custom_call_target="tpu_custom_call" | custom-call | flops 2097152 | bytes 2097152 | tf_op jit(solution)/shard_map/prepare/pallas_call | solution.py:230
  6.3 0.0 collective-permute-done.refs_1_
  6.3 0.0 collective-permute-done.1.refs_2_
  6.3 1.5 %collective-permute-done.2.refs_3_ = bf16[64,512]{1,0:T(8,128)(2,1)S(1)} collective-permute-done((bf16[64,512]{1,0:T(8,128)(2,1)S(1)}, bf16[64,512]{1,0:T(8,128)(2,1)S(1)}, u32[]{:S(2)}, u32[]{:S(2)}) %collective-permute-start.2) | collective-permute-done | bytes 65568 | tf_op jit(solution)/shard_map/ppermute | solution.py:228
  7.8 1.2 %spectra.1 = bf16[1152,128]{1,0:T(8,128)(2,1)S(1)} custom-call(bf16[64,512]{1,0:T(8,128)(2,1)S(1)} %get-tuple-element.12.refs_0_, bf16[64,512]{1,0:T(8,128)(2,1)S(1)} %collective-permute-done.refs_1_, bf16[64,512]{1,0:T(8,128)(2,1)S(1)} %collective-permute-done.1.refs_2_, bf16[64,512]{1,0:T(8,128)(2,1)S(1)} %collective-permute-done.2.refs_3_, ...), custom_call_target="tpu_custom_call" | custom-call | tf_op jit(solution)/shard_map/spectra/pallas_call | solution.py:243
  9.0 16.6 %all_to_all.10 = bf16[32,9,4,128]{3,2,1,0:T(4,128)(2,1)S(1)} all-to-all(bf16[32,9,4,128]{3,2,1,0:T(4,128)(2,1)S(1)} %bitcast.8), channel_id=1, replica_groups=mesh['region'=4,'slab'=8] {'slab','region'}, dimensions={0} | all-to-all | bytes 589824 | tf_op jit(solution)/shard_map/all_to_all | solution.py:252
  25.6 1.7 %cross.1 = bf16[32,64,128]{2,1,0:T(8,128)(2,1)S(1)} custom-call(bf16[1152,128]{1,0:T(8,128)(2,1)S(1)} %bitcast.9), custom_call_target="tpu_custom_call" | custom-call | tf_op jit(solution)/shard_map/cross/pallas_call | solution.py:253
  27.3 17.7 %all_to_all.11.in_ref = bf16[32,64,128]{2,1,0:T(8,128)(2,1)S(1)} all-to-all(bf16[32,64,128]{2,1,0:T(8,128)(2,1)S(1)} %cross.1), channel_id=1, replica_groups=mesh['region'=4,'slab'=8] {'slab','region'}, dimensions={0} | all-to-all | bytes 1048576 | tf_op jit(solution)/shard_map/all_to_all | solution.py:262
  45.0 1.1 %place.1 = bf16[128,2048]{1,0:T(8,128)(2,1)} custom-call(bf16[32,64,128]{2,1,0:T(8,128)(2,1)S(1)} %all_to_all.11.in_ref), custom_call_target="tpu_custom_call" | custom-call | tf_op jit(solution)/shard_map/place/pallas_call | solution.py:263
  (1 shorter events, 0.0 us)
Async XLA Ops:
  0.0 0.9 %copy-start.1 = (bf16[256,512]{1,0:T(8,128)(2,1)S(1)}, bf16[256,512]{1,0:T(8,128)(2,1)}, u32[]{:S(2)}) copy-start(bf16[256,512]{1,0:T(8,128)(2,1)} %records_ref.1) | copy-start | bytes 786436
  1.0 5.3 %collective-permute-start = (bf16[64,512]{1,0:T(8,128)(2,1)S(1)}, bf16[64,512]{1,0:T(8,128)(2,1)S(1)}, u32[]{:S(2)}, u32[]{:S(2)}) collective-permute-start(bf16[64,512]{1,0:T(8,128)(2,1)S(1)} %get-tuple-element.13), channel_id=1, source_target_pairs={{0,1},{1,0},{2,3},{3,2},{4,5},{5,4},{6,7},{7,6},{8,9},{9,8},{10,11... | collective-permute-start | bytes 196616 | tf_op jit(solution)/shard_map/ppermute | solution.py:228
  1.1 5.2 %collective-permute-start.1 = (bf16[64,512]{1,0:T(8,128)(2,1)S(1)}, bf16[64,512]{1,0:T(8,128)(2,1)S(1)}, u32[]{:S(2)}, u32[]{:S(2)}) collective-permute-start(bf16[64,512]{1,0:T(8,128)(2,1)S(1)} %get-tuple-element.14), channel_id=1, source_target_pairs={{0,2},{1,3},{2,0},{3,1},{4,6},{5,7},{6,4},{7,5},{8,10},{9,11},{10,... | collective-permute-start | bytes 196616 | tf_op jit(solution)/shard_map/ppermute | solution.py:228
  3.8 4.0 %collective-permute-start.2 = (bf16[64,512]{1,0:T(8,128)(2,1)S(1)}, bf16[64,512]{1,0:T(8,128)(2,1)S(1)}, u32[]{:S(2)}, u32[]{:S(2)}) collective-permute-start(bf16[64,512]{1,0:T(8,128)(2,1)S(1)} %get-tuple-element.15), channel_id=1, source_target_pairs={{0,3},{1,2},{2,1},{3,0},{4,7},{5,6},{6,5},{7,4},{8,11},{9,10},{10,... | collective-permute-start | bytes 196616 | tf_op jit(solution)/shard_map/ppermute | solution.py:228
  4.5 1.0 %copy-start = (f32[200,512]{1,0:T(8,128)S(1)}, f32[200,512]{1,0:T(8,128)}, u32[]{:S(2)}) copy-start(f32[200,512]{1,0:T(8,128)} %constant.6.clone.rows_ref) | copy-start | bytes 1228804

commit v6 on v5

--- a/solution.py
+++ b/solution.py
@@ -21,7 +21,14 @@
 TAPER_ROWS = 8
 EXACT = 256
 AXES = ("region", "slab")
-RANKS = ("slab", "region")
+SPECTRA_RANKS = [
+    16, 8, 24, 0, 15, 23, 7, 31, 26, 10, 18, 2, 19, 11, 27, 3,
+    20, 13, 28, 4, 21, 12, 29, 5, 22, 14, 30, 6, 17, 9, 25, 1,
+]
+RESULT_RANKS = [
+    0, 8, 16, 24, 2, 18, 10, 26, 7, 15, 23, 31, 3, 11, 19, 27,
+    4, 12, 20, 28, 17, 13, 21, 29, 6, 14, 22, 30, 1, 9, 5, 25,
+]
 
 
 def constant_rows():
@@ -152,7 +159,7 @@
     per_step = 2
     for region in range(regions):
         for segment in range(SEG):
-            sources = [((segment * parts + part) * regions + region) * rows for part in range(parts)]
+            sources = [SPECTRA_RANKS.index(region * slabs + segment * parts + part) * rows for part in range(parts)]
             block = jnp.concatenate([table_ref[at : at + count, :] for at in sources], axis=0).T
             at = region * LANES + segment * 2 * bins
             for half in (0, 1):
@@ -164,8 +171,9 @@
     one, zero = jnp.ones((), jnp.bfloat16), jnp.zeros((), jnp.bfloat16)
     for i in range(devices // per_step):
         home, first_slab = i % regions, i // regions * per_step
-        owners = [(first_slab + k) * regions + home for k in range(per_step)]
-        named = [table_ref[owner * rows + count : (owner + 1) * rows, :] for owner in owners]
+        owners = [home * slabs + first_slab + k for k in range(per_step)]
+        places = [SPECTRA_RANKS.index(owner) * rows for owner in owners]
+        named = [table_ref[at + count : at + rows, :] for at in places]
         named = jnp.concatenate(named, axis=1)
         first, second, target = named[0:1], named[1:2], named[2:3].astype(jnp.float32)
         own = flipped_ref[home * LANES : (home + 1) * LANES, :]
@@ -186,8 +194,9 @@
         real_sum = (real_sum * (1.0 / SEG)).astype(jnp.bfloat16)
         imag_sum = (imag_sum * (1.0 / SEG)).astype(jnp.bfloat16)
         for k, owner in enumerate(owners):
-            out_ref[owner, :bins, :] = real_sum[:, k * LANES : (k + 1) * LANES]
-            out_ref[owner, bins:, :] = imag_sum[:, k * LANES : (k + 1) * LANES]
+            at = RESULT_RANKS.index(owner)
+            out_ref[at, :bins, :] = real_sum[:, k * LANES : (k + 1) * LANES]
+            out_ref[at, bins:, :] = imag_sum[:, k * LANES : (k + 1) * LANES]
 
 
 def place_kernel(in_ref, out_ref):
@@ -199,7 +208,8 @@
     for kind in (0, 1):
         for j in range(devices // CLASSES):
             sources = range(j, devices, devices // CLASSES)
-            block = jnp.concatenate([in_ref[u, kind * bins : (kind + 1) * bins, :] for u in sources], axis=0).T
+            places = [RESULT_RANKS.index(SPECTRA_RANKS[u]) for u in sources]
+            block = jnp.concatenate([in_ref[at, kind * bins : (kind + 1) * bins, :] for at in places], axis=0).T
             natural = jnp.dot(block, order, preferred_element_type=jnp.float32)
             place = kind * BINS + j * LANES
             out_ref[:, place : place + LANES] = natural.astype(jnp.bfloat16)
@@ -249,7 +259,7 @@
         name="spectra",
     )(*arrived, *prepared)
     blocks = sent.reshape(devices, (count + INDEX_ROWS) // INDEX_ROWS, INDEX_ROWS, LANES)
-    table = lax.all_to_all(blocks, RANKS, split_axis=0, concat_axis=0, tiled=True).reshape(sent.shape)
+    table = lax.all_to_all(blocks, AXES, split_axis=0, concat_axis=0, tiled=True, axis_index_groups=[SPECTRA_RANKS]).reshape(sent.shape)
     partial = pl.pallas_call(
         functools.partial(cross_kernel, regions, slabs),
         out_shape=jax.ShapeDtypeStruct((devices, LANES // 2, pair_count), jnp.bfloat16),
@@ -259,7 +269,7 @@
         compiler_params=limit,
         name="cross",
     )(table)
-    pieces = lax.all_to_all(partial, RANKS, split_axis=0, concat_axis=0, tiled=True)
+    pieces = lax.all_to_all(partial, AXES, split_axis=0, concat_axis=0, tiled=True, axis_index_groups=[RESULT_RANKS])
     return pl.pallas_call(
         place_kernel,
         out_shape=jax.ShapeDtypeStruct((pair_count, 2 * BINS), jnp.bfloat16),
@@ -337,6 +347,7 @@
     devices = lax.axis_size("region") * slabs
     fits = (
         devices * LANES == 4 * BINS
+        and devices == len(SPECTRA_RANKS)
         and records.shape == (EXACT, NFFT * SEG // slabs)
         and slabs == 4 * SEG
         and first_station.shape[0] == LANES

time: 46.4 us -> 45.4 us (0.978)
  blocking collectives: 34.3 us -> 33.3 us
    all_to_all x2, blocking collectives: 34.3 us -> 33.3 us  [the longest x1 16.8 us: by_bins(): lax.all_to_all(partial, AXES, split_axis=0, concat_axis=0, tiled=True, ax...]
  transfers between devices with their start and end apart: 3 -> 3, of which waited for: 1 -> 1; matrix products, arithmetic and copies ran while one was open for 1% -> 2% of each run, Pallas kernels for 2% -> 2%
where the time goes in v6:
time: 45.4 us; the launch traced here: 45.2 us
  blocking collectives  33.3 us (73%)
  Pallas kernels  4.83 us (11%)
  starting transfers between devices  2.84 us (6%)
  local copies, waits for them, and re-layouts  1.95 us (4%)
  waiting for transfers between devices  1.49 us (3%)
  other arithmetic  0.69 us (2%)
    all_to_all x1, blocking collectives, by_bins(): lax.all_to_all(partial, AXES, split_axis=0, concat_axis=0, tiled=True, ax...  16.8 us
    all_to_all x1, blocking collectives, by_bins(): lax.all_to_all(blocks, AXES, split_axis=0, concat_axis=0, tiled=True, axi...  16.6 us
    ppermute x3, starting transfers between devices, by_bins(): lax.ppermute(divided[k], 'slab', [(i, i ^ k) for i in range(slabs)])  2.84 us
    unnamed x4, local copies, waits for them, and re-layouts  1.95 us
    pallas_call x1, Pallas kernels, by_bins(): pl.pallas_call(functools.partial(cross_kernel, regions, slabs), out_shape...  1.66 us
    ppermute x3, waiting for transfers between devices, by_bins(): lax.ppermute(divided[k], 'slab', [(i, i ^ k) for i in range(slabs)])  1.49 us
    pallas_call x1, Pallas kernels, by_bins(): pl.pallas_call(spectra_kernel, out_shape=jax.ShapeDtypeStruct((devices *...  1.22 us
    pallas_call x1, Pallas kernels, by_bins(): pl.pallas_call(place_kernel, out_shape=jax.ShapeDtypeStruct((pair_count,...  1.13 us
  transfers between devices with their start and end apart: 3, of which 1 were waited for; matrix products, arithmetic and copies ran while one was open for 2% of the time, Pallas kernels for 2%

profile of v6, /device:TPU:1, one launch (start us, length us, event | category | flops | bytes accessed | tf_op | source)
XLA Modules:
  0.0 45.2 jit_solution(1646791388345338658)
XLA Ops:
  0.0 0.0 copy-start.1
  0.0 0.9 %copy-done.1 = bf16[256,512]{1,0:T(8,128)(2,1)S(1)} copy-done((bf16[256,512]{1,0:T(8,128)(2,1)S(1)}, bf16[256,512]{1,0:T(8,128)(2,1)}, u32[]{:S(2)}) %copy-start.1) | copy-done | bytes 262168
  1.0 0.1 collective-permute-start
  1.1 2.7 %collective-permute-start.1 = (bf16[64,512]{1,0:T(8,128)(2,1)S(1)}, bf16[64,512]{1,0:T(8,128)(2,1)S(1)}, u32[]{:S(2)}, u32[]{:S(2)}) collective-permute-start(bf16[64,512]{1,0:T(8,128)(2,1)S(1)} %get-tuple-element.14), channel_id=1, source_target_pairs={{0,2},{1,3},{2,0},{3,1},{4,6},{5,7},{6,4},{7,5},{8,10},{9,11},{10,... | collective-permute-start | bytes 196616 | tf_op jit(solution)/shard_map/ppermute | solution.py:238
  3.8 0.0 collective-permute-start.2
  3.8 0.7 %fusion.named_ref = s32[1,128]{1,0:T(1,128)S(1)} fusion(s32[128,1]{0,1:T(1,128)} %param.7, s32[128]{0:T(128)} %param.6, s32[128]{0:T(128)} %param.8), kind=kLoop, calls=%fused_computation.1 | loop fusion | flops 512 | bytes 2048 | tf_op jit(solution)/shard_map/reshape | solution.py:252
  4.5 0.0 copy-start
  4.5 1.0 %copy-done = f32[200,512]{1,0:T(8,128)S(1)} copy-done((f32[200,512]{1,0:T(8,128)S(1)}, f32[200,512]{1,0:T(8,128)}, u32[]{:S(2)}) %copy-start) | copy-done | bytes 409624
  5.5 0.8 %prepare.1 = (bf16[4,128]{1,0:T(4,128)(2,1)S(1)}, f32[8,512]{1,0:T(8,128)S(1)}, bf16[2048,512]{1,0:T(8,128)(2,1)S(1)}) custom-call(s32[1,128]{1,0:T(1,128)S(1)} %fusion.named_ref, f32[200,512]{1,0:T(8,128)S(1)} %copy-done), custom_call_target="tpu_custom_call" | custom-call | flops 2097152 | bytes 2097152 | tf_op jit(solution)/shard_map/prepare/pallas_call | solution.py:240
  6.3 0.0 collective-permute-done.refs_1_
  6.3 0.0 collective-permute-done.1.refs_2_
  6.3 1.5 %collective-permute-done.2.refs_3_ = bf16[64,512]{1,0:T(8,128)(2,1)S(1)} collective-permute-done((bf16[64,512]{1,0:T(8,128)(2,1)S(1)}, bf16[64,512]{1,0:T(8,128)(2,1)S(1)}, u32[]{:S(2)}, u32[]{:S(2)}) %collective-permute-start.2) | collective-permute-done | bytes 65568 | tf_op jit(solution)/shard_map/ppermute | solution.py:238
  7.8 1.2 %spectra.1 = bf16[1152,128]{1,0:T(8,128)(2,1)S(1)} custom-call(bf16[64,512]{1,0:T(8,128)(2,1)S(1)} %get-tuple-element.12.refs_0_, bf16[64,512]{1,0:T(8,128)(2,1)S(1)} %collective-permute-done.refs_1_, bf16[64,512]{1,0:T(8,128)(2,1)S(1)} %collective-permute-done.1.refs_2_, bf16[64,512]{1,0:T(8,128)(2,1)S(1)} %collective-permute-done.2.refs_3_, ...), custom_call_target="tpu_custom_call" | custom-call | tf_op jit(solution)/shard_map/spectra/pallas_call | solution.py:253
  9.0 16.6 %all_to_all.10 = bf16[32,9,4,128]{3,2,1,0:T(4,128)(2,1)S(1)} all-to-all(bf16[32,9,4,128]{3,2,1,0:T(4,128)(2,1)S(1)} %bitcast.8), channel_id=1, replica_groups={{16,8,24,0,15,23,7,31,26,10,18,2,19,11,27,3,20,13,28,4,21,12,29,5,22,14..., dimensions={0} | all-to-all | bytes 589824 | tf_op jit(solution)/shard_map/all_to_all | solution.py:262
  25.6 1.7 %cross.1 = bf16[32,64,128]{2,1,0:T(8,128)(2,1)S(1)} custom-call(bf16[1152,128]{1,0:T(8,128)(2,1)S(1)} %bitcast.9), custom_call_target="tpu_custom_call" | custom-call | tf_op jit(solution)/shard_map/cross/pallas_call | solution.py:263
  27.3 16.8 %all_to_all.11.in_ref = bf16[32,64,128]{2,1,0:T(8,128)(2,1)S(1)} all-to-all(bf16[32,64,128]{2,1,0:T(8,128)(2,1)S(1)} %cross.1), channel_id=1, replica_groups={{0,8,16,24,2,18,10,26,7,15,23,31,3,11,19,27,4,12,20,28,17,13,21,29,6,14..., dimensions={0} | all-to-all | bytes 1048576 | tf_op jit(solution)/shard_map/all_to_all | solution.py:272
  44.0 1.1 %place.1 = bf16[128,2048]{1,0:T(8,128)(2,1)} custom-call(bf16[32,64,128]{2,1,0:T(8,128)(2,1)S(1)} %all_to_all.11.in_ref), custom_call_target="tpu_custom_call" | custom-call | tf_op jit(solution)/shard_map/place/pallas_call | solution.py:273
  (1 shorter events, 0.0 us)
Async XLA Ops:
  0.0 0.9 %copy-start.1 = (bf16[256,512]{1,0:T(8,128)(2,1)S(1)}, bf16[256,512]{1,0:T(8,128)(2,1)}, u32[]{:S(2)}) copy-start(bf16[256,512]{1,0:T(8,128)(2,1)} %records_ref.1) | copy-start | bytes 786436
  1.0 5.3 %collective-permute-start = (bf16[64,512]{1,0:T(8,128)(2,1)S(1)}, bf16[64,512]{1,0:T(8,128)(2,1)S(1)}, u32[]{:S(2)}, u32[]{:S(2)}) collective-permute-start(bf16[64,512]{1,0:T(8,128)(2,1)S(1)} %get-tuple-element.13), channel_id=1, source_target_pairs={{0,1},{1,0},{2,3},{3,2},{4,5},{5,4},{6,7},{7,6},{8,9},{9,8},{10,11... | collective-permute-start | bytes 196616 | tf_op jit(solution)/shard_map/ppermute | solution.py:238
  1.1 5.2 %collective-permute-start.1 = (bf16[64,512]{1,0:T(8,128)(2,1)S(1)}, bf16[64,512]{1,0:T(8,128)(2,1)S(1)}, u32[]{:S(2)}, u32[]{:S(2)}) collective-permute-start(bf16[64,512]{1,0:T(8,128)(2,1)S(1)} %get-tuple-element.14), channel_id=1, source_target_pairs={{0,2},{1,3},{2,0},{3,1},{4,6},{5,7},{6,4},{7,5},{8,10},{9,11},{10,... | collective-permute-start | bytes 196616 | tf_op jit(solution)/shard_map/ppermute | solution.py:238
  3.8 4.0 %collective-permute-start.2 = (bf16[64,512]{1,0:T(8,128)(2,1)S(1)}, bf16[64,512]{1,0:T(8,128)(2,1)S(1)}, u32[]{:S(2)}, u32[]{:S(2)}) collective-permute-start(bf16[64,512]{1,0:T(8,128)(2,1)S(1)} %get-tuple-element.15), channel_id=1, source_target_pairs={{0,3},{1,2},{2,1},{3,0},{4,7},{5,6},{6,5},{7,4},{8,11},{9,10},{10,... | collective-permute-start | bytes 196616 | tf_op jit(solution)/shard_map/ppermute | solution.py:238
  4.5 1.0 %copy-start = (f32[200,512]{1,0:T(8,128)S(1)}, f32[200,512]{1,0:T(8,128)}, u32[]{:S(2)}) copy-start(f32[200,512]{1,0:T(8,128)} %constant.6.clone.rows_ref) | copy-start | bytes 1228804

commit v7 on v6

--- a/solution.py
+++ b/solution.py
@@ -26,8 +26,8 @@
     20, 13, 28, 4, 21, 12, 29, 5, 22, 14, 30, 6, 17, 9, 25, 1,
 ]
 RESULT_RANKS = [
-    0, 8, 16, 24, 2, 18, 10, 26, 7, 15, 23, 31, 3, 11, 19, 27,
-    4, 12, 20, 28, 17, 13, 21, 29, 6, 14, 22, 30, 1, 9, 5, 25,
+    16, 0, 8, 24, 2, 18, 10, 26, 15, 23, 7, 31, 3, 11, 19, 27,
+    4, 12, 25, 28, 17, 13, 21, 29, 6, 14, 22, 30, 1, 9, 5, 20,
 ]
 
 

time: 45.4 us -> 45 us (level)
  blocking collectives: 33.3 us -> 32.6 us
    all_to_all x1, blocking collectives: 16.8 us -> 16.1 us  [by_bins(): lax.all_to_all(partial, AXES, split_axis=0, concat_axis=0, tiled=True, ax...]
where the time goes in v7:
time: 45 us; the launch traced here: 44.5 us
  blocking collectives  32.6 us (72%)
  Pallas kernels  4.83 us (11%)
  starting transfers between devices  2.84 us (6%)
  local copies, waits for them, and re-layouts  1.95 us (4%)
  waiting for transfers between devices  1.49 us (3%)
  other arithmetic  0.69 us (2%)
    all_to_all x1, blocking collectives, by_bins(): lax.all_to_all(blocks, AXES, split_axis=0, concat_axis=0, tiled=True, axi...  16.6 us
    all_to_all x1, blocking collectives, by_bins(): lax.all_to_all(partial, AXES, split_axis=0, concat_axis=0, tiled=True, ax...  16.1 us
    ppermute x3, starting transfers between devices, by_bins(): lax.ppermute(divided[k], 'slab', [(i, i ^ k) for i in range(slabs)])  2.84 us
    unnamed x4, local copies, waits for them, and re-layouts  1.95 us
    pallas_call x1, Pallas kernels, by_bins(): pl.pallas_call(functools.partial(cross_kernel, regions, slabs), out_shape...  1.66 us
    ppermute x3, waiting for transfers between devices, by_bins(): lax.ppermute(divided[k], 'slab', [(i, i ^ k) for i in range(slabs)])  1.49 us
    pallas_call x1, Pallas kernels, by_bins(): pl.pallas_call(spectra_kernel, out_shape=jax.ShapeDtypeStruct((devices *...  1.22 us
    pallas_call x1, Pallas kernels, by_bins(): pl.pallas_call(place_kernel, out_shape=jax.ShapeDtypeStruct((pair_count,...  1.13 us
  transfers between devices with their start and end apart: 3, of which 1 were waited for; matrix products, arithmetic and copies ran while one was open for 2% of the time, Pallas kernels for 2%

profile of v7, /device:TPU:1, one launch (start us, length us, event | category | flops | bytes accessed | tf_op | source)
XLA Modules:
  0.0 44.5 jit_solution(7983078526922369160)
XLA Ops:
  0.0 0.0 copy-start.1
  0.0 0.9 %copy-done.1 = bf16[256,512]{1,0:T(8,128)(2,1)S(1)} copy-done((bf16[256,512]{1,0:T(8,128)(2,1)S(1)}, bf16[256,512]{1,0:T(8,128)(2,1)}, u32[]{:S(2)}) %copy-start.1) | copy-done | bytes 262168
  1.0 0.1 collective-permute-start
  1.1 2.7 %collective-permute-start.1 = (bf16[64,512]{1,0:T(8,128)(2,1)S(1)}, bf16[64,512]{1,0:T(8,128)(2,1)S(1)}, u32[]{:S(2)}, u32[]{:S(2)}) collective-permute-start(bf16[64,512]{1,0:T(8,128)(2,1)S(1)} %get-tuple-element.14), channel_id=1, source_target_pairs={{0,2},{1,3},{2,0},{3,1},{4,6},{5,7},{6,4},{7,5},{8,10},{9,11},{10,... | collective-permute-start | bytes 196616 | tf_op jit(solution)/shard_map/ppermute | solution.py:238
  3.8 0.0 collective-permute-start.2
  3.8 0.7 %fusion.named_ref = s32[1,128]{1,0:T(1,128)S(1)} fusion(s32[128,1]{0,1:T(1,128)} %param.7, s32[128]{0:T(128)} %param.6, s32[128]{0:T(128)} %param.8), kind=kLoop, calls=%fused_computation.1 | loop fusion | flops 512 | bytes 2048 | tf_op jit(solution)/shard_map/reshape | solution.py:252
  4.5 0.0 copy-start
  4.5 1.0 %copy-done = f32[200,512]{1,0:T(8,128)S(1)} copy-done((f32[200,512]{1,0:T(8,128)S(1)}, f32[200,512]{1,0:T(8,128)}, u32[]{:S(2)}) %copy-start) | copy-done | bytes 409624
  5.5 0.8 %prepare.1 = (bf16[4,128]{1,0:T(4,128)(2,1)S(1)}, f32[8,512]{1,0:T(8,128)S(1)}, bf16[2048,512]{1,0:T(8,128)(2,1)S(1)}) custom-call(s32[1,128]{1,0:T(1,128)S(1)} %fusion.named_ref, f32[200,512]{1,0:T(8,128)S(1)} %copy-done), custom_call_target="tpu_custom_call" | custom-call | flops 2097152 | bytes 2097152 | tf_op jit(solution)/shard_map/prepare/pallas_call | solution.py:240
  6.3 0.0 collective-permute-done.refs_1_
  6.3 0.0 collective-permute-done.1.refs_2_
  6.3 1.5 %collective-permute-done.2.refs_3_ = bf16[64,512]{1,0:T(8,128)(2,1)S(1)} collective-permute-done((bf16[64,512]{1,0:T(8,128)(2,1)S(1)}, bf16[64,512]{1,0:T(8,128)(2,1)S(1)}, u32[]{:S(2)}, u32[]{:S(2)}) %collective-permute-start.2) | collective-permute-done | bytes 65568 | tf_op jit(solution)/shard_map/ppermute | solution.py:238
  7.8 1.2 %spectra.1 = bf16[1152,128]{1,0:T(8,128)(2,1)S(1)} custom-call(bf16[64,512]{1,0:T(8,128)(2,1)S(1)} %get-tuple-element.12.refs_0_, bf16[64,512]{1,0:T(8,128)(2,1)S(1)} %collective-permute-done.refs_1_, bf16[64,512]{1,0:T(8,128)(2,1)S(1)} %collective-permute-done.1.refs_2_, bf16[64,512]{1,0:T(8,128)(2,1)S(1)} %collective-permute-done.2.refs_3_, ...), custom_call_target="tpu_custom_call" | custom-call | tf_op jit(solution)/shard_map/spectra/pallas_call | solution.py:253
  9.0 16.6 %all_to_all.10 = bf16[32,9,4,128]{3,2,1,0:T(4,128)(2,1)S(1)} all-to-all(bf16[32,9,4,128]{3,2,1,0:T(4,128)(2,1)S(1)} %bitcast.8), channel_id=1, replica_groups={{16,8,24,0,15,23,7,31,26,10,18,2,19,11,27,3,20,13,28,4,21,12,29,5,22,14..., dimensions={0} | all-to-all | bytes 589824 | tf_op jit(solution)/shard_map/all_to_all | solution.py:262
  25.6 1.7 %cross.1 = bf16[32,64,128]{2,1,0:T(8,128)(2,1)S(1)} custom-call(bf16[1152,128]{1,0:T(8,128)(2,1)S(1)} %bitcast.9), custom_call_target="tpu_custom_call" | custom-call | tf_op jit(solution)/shard_map/cross/pallas_call | solution.py:263
  27.3 16.1 %all_to_all.11.in_ref = bf16[32,64,128]{2,1,0:T(8,128)(2,1)S(1)} all-to-all(bf16[32,64,128]{2,1,0:T(8,128)(2,1)S(1)} %cross.1), channel_id=1, replica_groups={{16,0,8,24,2,18,10,26,15,23,7,31,3,11,19,27,4,12,25,28,17,13,21,29,6,14..., dimensions={0} | all-to-all | bytes 1048576 | tf_op jit(solution)/shard_map/all_to_all | solution.py:272
  43.3 1.1 %place.1 = bf16[128,2048]{1,0:T(8,128)(2,1)} custom-call(bf16[32,64,128]{2,1,0:T(8,128)(2,1)S(1)} %all_to_all.11.in_ref), custom_call_target="tpu_custom_call" | custom-call | tf_op jit(solution)/shard_map/place/pallas_call | solution.py:273
  (1 shorter events, 0.0 us)
Async XLA Ops:
  0.0 0.9 %copy-start.1 = (bf16[256,512]{1,0:T(8,128)(2,1)S(1)}, bf16[256,512]{1,0:T(8,128)(2,1)}, u32[]{:S(2)}) copy-start(bf16[256,512]{1,0:T(8,128)(2,1)} %records_ref.1) | copy-start | bytes 786436
  1.0 5.3 %collective-permute-start = (bf16[64,512]{1,0:T(8,128)(2,1)S(1)}, bf16[64,512]{1,0:T(8,128)(2,1)S(1)}, u32[]{:S(2)}, u32[]{:S(2)}) collective-permute-start(bf16[64,512]{1,0:T(8,128)(2,1)S(1)} %get-tuple-element.13), channel_id=1, source_target_pairs={{0,1},{1,0},{2,3},{3,2},{4,5},{5,4},{6,7},{7,6},{8,9},{9,8},{10,11... | collective-permute-start | bytes 196616 | tf_op jit(solution)/shard_map/ppermute | solution.py:238
  1.1 5.2 %collective-permute-start.1 = (bf16[64,512]{1,0:T(8,128)(2,1)S(1)}, bf16[64,512]{1,0:T(8,128)(2,1)S(1)}, u32[]{:S(2)}, u32[]{:S(2)}) collective-permute-start(bf16[64,512]{1,0:T(8,128)(2,1)S(1)} %get-tuple-element.14), channel_id=1, source_target_pairs={{0,2},{1,3},{2,0},{3,1},{4,6},{5,7},{6,4},{7,5},{8,10},{9,11},{10,... | collective-permute-start | bytes 196616 | tf_op jit(solution)/shard_map/ppermute | solution.py:238
  3.8 4.0 %collective-permute-start.2 = (bf16[64,512]{1,0:T(8,128)(2,1)S(1)}, bf16[64,512]{1,0:T(8,128)(2,1)S(1)}, u32[]{:S(2)}, u32[]{:S(2)}) collective-permute-start(bf16[64,512]{1,0:T(8,128)(2,1)S(1)} %get-tuple-element.15), channel_id=1, source_target_pairs={{0,3},{1,2},{2,1},{3,0},{4,7},{5,6},{6,5},{7,4},{8,11},{9,10},{10,... | collective-permute-start | bytes 196616 | tf_op jit(solution)/shard_map/ppermute | solution.py:238
  4.5 1.0 %copy-start = (f32[200,512]{1,0:T(8,128)S(1)}, f32[200,512]{1,0:T(8,128)}, u32[]{:S(2)}) copy-start(f32[200,512]{1,0:T(8,128)} %constant.6.clone.rows_ref) | copy-start | bytes 1228804

commit v8 on v7

--- a/solution.py
+++ b/solution.py
@@ -22,12 +22,12 @@
 EXACT = 256
 AXES = ("region", "slab")
 SPECTRA_RANKS = [
-    16, 8, 24, 0, 15, 23, 7, 31, 26, 10, 18, 2, 19, 11, 27, 3,
-    20, 13, 28, 4, 21, 12, 29, 5, 22, 14, 30, 6, 17, 9, 25, 1,
+    24, 16, 8, 0, 15, 23, 7, 31, 26, 10, 18, 2, 19, 3, 11, 27,
+    20, 13, 28, 4, 17, 9, 25, 1, 22, 14, 30, 6, 21, 12, 29, 5,
 ]
 RESULT_RANKS = [
-    16, 0, 8, 24, 2, 18, 10, 26, 15, 23, 7, 31, 3, 11, 19, 27,
-    4, 12, 25, 28, 17, 13, 21, 29, 6, 14, 22, 30, 1, 9, 5, 20,
+    16, 0, 8, 24, 17, 13, 21, 29, 15, 23, 7, 31, 3, 11, 19, 27,
+    1, 9, 5, 20, 2, 18, 10, 26, 6, 14, 22, 30, 4, 12, 25, 28,
 ]
 
 

time: 45 us -> 45.1 us (level)
  no operation moved by 1% of the time
where the time goes in v8:
time: 45.1 us; the launch traced here: 44.9 us
  blocking collectives  33 us (73%)
  Pallas kernels  4.83 us (11%)
  starting transfers between devices  2.84 us (6%)
  local copies, waits for them, and re-layouts  1.95 us (4%)
  waiting for transfers between devices  1.49 us (3%)
  other arithmetic  0.69 us (2%)
    all_to_all x1, blocking collectives, by_bins(): lax.all_to_all(blocks, AXES, split_axis=0, concat_axis=0, tiled=True, axi...  16.9 us
    all_to_all x1, blocking collectives, by_bins(): lax.all_to_all(partial, AXES, split_axis=0, concat_axis=0, tiled=True, ax...  16.1 us
    ppermute x3, starting transfers between devices, by_bins(): lax.ppermute(divided[k], 'slab', [(i, i ^ k) for i in range(slabs)])  2.84 us
    unnamed x4, local copies, waits for them, and re-layouts  1.95 us
    pallas_call x1, Pallas kernels, by_bins(): pl.pallas_call(functools.partial(cross_kernel, regions, slabs), out_shape...  1.67 us
    ppermute x3, waiting for transfers between devices, by_bins(): lax.ppermute(divided[k], 'slab', [(i, i ^ k) for i in range(slabs)])  1.49 us
    pallas_call x1, Pallas kernels, by_bins(): pl.pallas_call(spectra_kernel, out_shape=jax.ShapeDtypeStruct((devices *...  1.22 us
    pallas_call x1, Pallas kernels, by_bins(): pl.pallas_call(place_kernel, out_shape=jax.ShapeDtypeStruct((pair_count,...  1.13 us
  transfers between devices with their start and end apart: 3, of which 1 were waited for; matrix products, arithmetic and copies ran while one was open for 2% of the time, Pallas kernels for 2%

profile of v8, /device:TPU:1, one launch (start us, length us, event | category | flops | bytes accessed | tf_op | source)
XLA Modules:
  0.0 44.9 jit_solution(4786407102780300964)
XLA Ops:
  0.0 0.0 copy-start.1
  0.0 0.9 %copy-done.1 = bf16[256,512]{1,0:T(8,128)(2,1)S(1)} copy-done((bf16[256,512]{1,0:T(8,128)(2,1)S(1)}, bf16[256,512]{1,0:T(8,128)(2,1)}, u32[]{:S(2)}) %copy-start.1) | copy-done | bytes 262168
  1.0 0.1 collective-permute-start
  1.1 2.7 %collective-permute-start.1 = (bf16[64,512]{1,0:T(8,128)(2,1)S(1)}, bf16[64,512]{1,0:T(8,128)(2,1)S(1)}, u32[]{:S(2)}, u32[]{:S(2)}) collective-permute-start(bf16[64,512]{1,0:T(8,128)(2,1)S(1)} %get-tuple-element.14), channel_id=1, source_target_pairs={{0,2},{1,3},{2,0},{3,1},{4,6},{5,7},{6,4},{7,5},{8,10},{9,11},{10,... | collective-permute-start | bytes 196616 | tf_op jit(solution)/shard_map/ppermute | solution.py:238
  3.8 0.0 collective-permute-start.2
  3.8 0.7 %fusion.named_ref = s32[1,128]{1,0:T(1,128)S(1)} fusion(s32[128,1]{0,1:T(1,128)} %param.7, s32[128]{0:T(128)} %param.6, s32[128]{0:T(128)} %param.8), kind=kLoop, calls=%fused_computation.1 | loop fusion | flops 512 | bytes 2048 | tf_op jit(solution)/shard_map/reshape | solution.py:252
  4.5 0.0 copy-start
  4.5 1.0 %copy-done = f32[200,512]{1,0:T(8,128)S(1)} copy-done((f32[200,512]{1,0:T(8,128)S(1)}, f32[200,512]{1,0:T(8,128)}, u32[]{:S(2)}) %copy-start) | copy-done | bytes 409624
  5.5 0.8 %prepare.1 = (bf16[4,128]{1,0:T(4,128)(2,1)S(1)}, f32[8,512]{1,0:T(8,128)S(1)}, bf16[2048,512]{1,0:T(8,128)(2,1)S(1)}) custom-call(s32[1,128]{1,0:T(1,128)S(1)} %fusion.named_ref, f32[200,512]{1,0:T(8,128)S(1)} %copy-done), custom_call_target="tpu_custom_call" | custom-call | flops 2097152 | bytes 2097152 | tf_op jit(solution)/shard_map/prepare/pallas_call | solution.py:240
  6.3 0.0 collective-permute-done.refs_1_
  6.3 0.0 collective-permute-done.1.refs_2_
  6.3 1.5 %collective-permute-done.2.refs_3_ = bf16[64,512]{1,0:T(8,128)(2,1)S(1)} collective-permute-done((bf16[64,512]{1,0:T(8,128)(2,1)S(1)}, bf16[64,512]{1,0:T(8,128)(2,1)S(1)}, u32[]{:S(2)}, u32[]{:S(2)}) %collective-permute-start.2) | collective-permute-done | bytes 65568 | tf_op jit(solution)/shard_map/ppermute | solution.py:238
  7.8 1.2 %spectra.1 = bf16[1152,128]{1,0:T(8,128)(2,1)S(1)} custom-call(bf16[64,512]{1,0:T(8,128)(2,1)S(1)} %get-tuple-element.12.refs_0_, bf16[64,512]{1,0:T(8,128)(2,1)S(1)} %collective-permute-done.refs_1_, bf16[64,512]{1,0:T(8,128)(2,1)S(1)} %collective-permute-done.1.refs_2_, bf16[64,512]{1,0:T(8,128)(2,1)S(1)} %collective-permute-done.2.refs_3_, ...), custom_call_target="tpu_custom_call" | custom-call | tf_op jit(solution)/shard_map/spectra/pallas_call | solution.py:253
  9.0 16.9 %all_to_all.10 = bf16[32,9,4,128]{3,2,1,0:T(4,128)(2,1)S(1)} all-to-all(bf16[32,9,4,128]{3,2,1,0:T(4,128)(2,1)S(1)} %bitcast.8), channel_id=1, replica_groups={{24,16,8,0,15,23,7,31,26,10,18,2,19,3,11,27,20,13,28,4,17,9,25,1,22,14,..., dimensions={0} | all-to-all | bytes 589824 | tf_op jit(solution)/shard_map/all_to_all | solution.py:262
  25.9 1.7 %cross.1 = bf16[32,64,128]{2,1,0:T(8,128)(2,1)S(1)} custom-call(bf16[1152,128]{1,0:T(8,128)(2,1)S(1)} %bitcast.9), custom_call_target="tpu_custom_call" | custom-call | tf_op jit(solution)/shard_map/cross/pallas_call | solution.py:263
  27.6 16.1 %all_to_all.11.in_ref = bf16[32,64,128]{2,1,0:T(8,128)(2,1)S(1)} all-to-all(bf16[32,64,128]{2,1,0:T(8,128)(2,1)S(1)} %cross.1), channel_id=1, replica_groups={{16,0,8,24,17,13,21,29,15,23,7,31,3,11,19,27,1,9,5,20,2,18,10,26,6,14,2..., dimensions={0} | all-to-all | bytes 1048576 | tf_op jit(solution)/shard_map/all_to_all | solution.py:272
  43.7 1.1 %place.1 = bf16[128,2048]{1,0:T(8,128)(2,1)} custom-call(bf16[32,64,128]{2,1,0:T(8,128)(2,1)S(1)} %all_to_all.11.in_ref), custom_call_target="tpu_custom_call" | custom-call | tf_op jit(solution)/shard_map/place/pallas_call | solution.py:273
  (1 shorter events, 0.0 us)
Async XLA Ops:
  0.0 0.9 %copy-start.1 = (bf16[256,512]{1,0:T(8,128)(2,1)S(1)}, bf16[256,512]{1,0:T(8,128)(2,1)}, u32[]{:S(2)}) copy-start(bf16[256,512]{1,0:T(8,128)(2,1)} %records_ref.1) | copy-start | bytes 786436
  1.0 5.3 %collective-permute-start = (bf16[64,512]{1,0:T(8,128)(2,1)S(1)}, bf16[64,512]{1,0:T(8,128)(2,1)S(1)}, u32[]{:S(2)}, u32[]{:S(2)}) collective-permute-start(bf16[64,512]{1,0:T(8,128)(2,1)S(1)} %get-tuple-element.13), channel_id=1, source_target_pairs={{0,1},{1,0},{2,3},{3,2},{4,5},{5,4},{6,7},{7,6},{8,9},{9,8},{10,11... | collective-permute-start | bytes 196616 | tf_op jit(solution)/shard_map/ppermute | solution.py:238
  1.1 5.2 %collective-permute-start.1 = (bf16[64,512]{1,0:T(8,128)(2,1)S(1)}, bf16[64,512]{1,0:T(8,128)(2,1)S(1)}, u32[]{:S(2)}, u32[]{:S(2)}) collective-permute-start(bf16[64,512]{1,0:T(8,128)(2,1)S(1)} %get-tuple-element.14), channel_id=1, source_target_pairs={{0,2},{1,3},{2,0},{3,1},{4,6},{5,7},{6,4},{7,5},{8,10},{9,11},{10,... | collective-permute-start | bytes 196616 | tf_op jit(solution)/shard_map/ppermute | solution.py:238
  3.8 4.0 %collective-permute-start.2 = (bf16[64,512]{1,0:T(8,128)(2,1)S(1)}, bf16[64,512]{1,0:T(8,128)(2,1)S(1)}, u32[]{:S(2)}, u32[]{:S(2)}) collective-permute-start(bf16[64,512]{1,0:T(8,128)(2,1)S(1)} %get-tuple-element.15), channel_id=1, source_target_pairs={{0,3},{1,2},{2,1},{3,0},{4,7},{5,6},{6,5},{7,4},{8,11},{9,10},{10,... | collective-permute-start | bytes 196616 | tf_op jit(solution)/shard_map/ppermute | solution.py:238
  4.5 1.0 %copy-start = (f32[200,512]{1,0:T(8,128)S(1)}, f32[200,512]{1,0:T(8,128)}, u32[]{:S(2)}) copy-start(f32[200,512]{1,0:T(8,128)} %constant.6.clone.rows_ref) | copy-start | bytes 1228804

commit v9 on v8

--- a/solution.py
+++ b/solution.py
@@ -26,8 +26,8 @@
     20, 13, 28, 4, 17, 9, 25, 1, 22, 14, 30, 6, 21, 12, 29, 5,
 ]
 RESULT_RANKS = [
-    16, 0, 8, 24, 17, 13, 21, 29, 15, 23, 7, 31, 3, 11, 19, 27,
-    1, 9, 5, 20, 2, 18, 10, 26, 6, 14, 22, 30, 4, 12, 25, 28,
+    16, 0, 8, 24, 2, 18, 10, 26, 15, 23, 7, 31, 3, 11, 19, 27,
+    4, 12, 25, 28, 17, 13, 21, 29, 6, 14, 22, 30, 1, 9, 5, 20,
 ]
 
 

time: 45.1 us -> 45 us (level)
  no operation moved by 1% of the time
where the time goes in v9:
time: 45 us; the launch traced here: 44.5 us
  blocking collectives  32.6 us (72%)
  Pallas kernels  4.83 us (11%)
  starting transfers between devices  2.84 us (6%)
  local copies, waits for them, and re-layouts  1.95 us (4%)
  waiting for transfers between devices  1.49 us (3%)
  other arithmetic  0.69 us (2%)
    all_to_all x1, blocking collectives, by_bins(): lax.all_to_all(blocks, AXES, split_axis=0, concat_axis=0, tiled=True, axi...  16.9 us
    all_to_all x1, blocking collectives, by_bins(): lax.all_to_all(partial, AXES, split_axis=0, concat_axis=0, tiled=True, ax...  15.7 us
    ppermute x3, starting transfers between devices, by_bins(): lax.ppermute(divided[k], 'slab', [(i, i ^ k) for i in range(slabs)])  2.84 us
    unnamed x4, local copies, waits for them, and re-layouts  1.95 us
    pallas_call x1, Pallas kernels, by_bins(): pl.pallas_call(functools.partial(cross_kernel, regions, slabs), out_shape...  1.67 us
    ppermute x3, waiting for transfers between devices, by_bins(): lax.ppermute(divided[k], 'slab', [(i, i ^ k) for i in range(slabs)])  1.49 us
    pallas_call x1, Pallas kernels, by_bins(): pl.pallas_call(spectra_kernel, out_shape=jax.ShapeDtypeStruct((devices *...  1.22 us
    pallas_call x1, Pallas kernels, by_bins(): pl.pallas_call(place_kernel, out_shape=jax.ShapeDtypeStruct((pair_count,...  1.13 us
  transfers between devices with their start and end apart: 3, of which 1 were waited for; matrix products, arithmetic and copies ran while one was open for 2% of the time, Pallas kernels for 2%

profile of v9, /device:TPU:1, one launch (start us, length us, event | category | flops | bytes accessed | tf_op | source)
XLA Modules:
  0.0 44.5 jit_solution(16120127652028681604)
XLA Ops:
  0.0 0.0 copy-start.1
  0.0 0.9 %copy-done.1 = bf16[256,512]{1,0:T(8,128)(2,1)S(1)} copy-done((bf16[256,512]{1,0:T(8,128)(2,1)S(1)}, bf16[256,512]{1,0:T(8,128)(2,1)}, u32[]{:S(2)}) %copy-start.1) | copy-done | bytes 262168
  1.0 0.1 collective-permute-start
  1.1 2.7 %collective-permute-start.1 = (bf16[64,512]{1,0:T(8,128)(2,1)S(1)}, bf16[64,512]{1,0:T(8,128)(2,1)S(1)}, u32[]{:S(2)}, u32[]{:S(2)}) collective-permute-start(bf16[64,512]{1,0:T(8,128)(2,1)S(1)} %get-tuple-element.14), channel_id=1, source_target_pairs={{0,2},{1,3},{2,0},{3,1},{4,6},{5,7},{6,4},{7,5},{8,10},{9,11},{10,... | collective-permute-start | bytes 196616 | tf_op jit(solution)/shard_map/ppermute | solution.py:238
  3.8 0.0 collective-permute-start.2
  3.8 0.7 %fusion.named_ref = s32[1,128]{1,0:T(1,128)S(1)} fusion(s32[128,1]{0,1:T(1,128)} %param.7, s32[128]{0:T(128)} %param.6, s32[128]{0:T(128)} %param.8), kind=kLoop, calls=%fused_computation.1 | loop fusion | flops 512 | bytes 2048 | tf_op jit(solution)/shard_map/reshape | solution.py:252
  4.5 0.0 copy-start
  4.5 1.0 %copy-done = f32[200,512]{1,0:T(8,128)S(1)} copy-done((f32[200,512]{1,0:T(8,128)S(1)}, f32[200,512]{1,0:T(8,128)}, u32[]{:S(2)}) %copy-start) | copy-done | bytes 409624
  5.5 0.8 %prepare.1 = (bf16[4,128]{1,0:T(4,128)(2,1)S(1)}, f32[8,512]{1,0:T(8,128)S(1)}, bf16[2048,512]{1,0:T(8,128)(2,1)S(1)}) custom-call(s32[1,128]{1,0:T(1,128)S(1)} %fusion.named_ref, f32[200,512]{1,0:T(8,128)S(1)} %copy-done), custom_call_target="tpu_custom_call" | custom-call | flops 2097152 | bytes 2097152 | tf_op jit(solution)/shard_map/prepare/pallas_call | solution.py:240
  6.3 0.0 collective-permute-done.refs_1_
  6.3 0.0 collective-permute-done.1.refs_2_
  6.3 1.5 %collective-permute-done.2.refs_3_ = bf16[64,512]{1,0:T(8,128)(2,1)S(1)} collective-permute-done((bf16[64,512]{1,0:T(8,128)(2,1)S(1)}, bf16[64,512]{1,0:T(8,128)(2,1)S(1)}, u32[]{:S(2)}, u32[]{:S(2)}) %collective-permute-start.2) | collective-permute-done | bytes 65568 | tf_op jit(solution)/shard_map/ppermute | solution.py:238
  7.8 1.2 %spectra.1 = bf16[1152,128]{1,0:T(8,128)(2,1)S(1)} custom-call(bf16[64,512]{1,0:T(8,128)(2,1)S(1)} %get-tuple-element.12.refs_0_, bf16[64,512]{1,0:T(8,128)(2,1)S(1)} %collective-permute-done.refs_1_, bf16[64,512]{1,0:T(8,128)(2,1)S(1)} %collective-permute-done.1.refs_2_, bf16[64,512]{1,0:T(8,128)(2,1)S(1)} %collective-permute-done.2.refs_3_, ...), custom_call_target="tpu_custom_call" | custom-call | tf_op jit(solution)/shard_map/spectra/pallas_call | solution.py:253
  9.0 16.9 %all_to_all.10 = bf16[32,9,4,128]{3,2,1,0:T(4,128)(2,1)S(1)} all-to-all(bf16[32,9,4,128]{3,2,1,0:T(4,128)(2,1)S(1)} %bitcast.8), channel_id=1, replica_groups={{24,16,8,0,15,23,7,31,26,10,18,2,19,3,11,27,20,13,28,4,17,9,25,1,22,14,..., dimensions={0} | all-to-all | bytes 589824 | tf_op jit(solution)/shard_map/all_to_all | solution.py:262
  25.9 1.7 %cross.1 = bf16[32,64,128]{2,1,0:T(8,128)(2,1)S(1)} custom-call(bf16[1152,128]{1,0:T(8,128)(2,1)S(1)} %bitcast.9), custom_call_target="tpu_custom_call" | custom-call | tf_op jit(solution)/shard_map/cross/pallas_call | solution.py:263
  27.6 15.7 %all_to_all.11.in_ref = bf16[32,64,128]{2,1,0:T(8,128)(2,1)S(1)} all-to-all(bf16[32,64,128]{2,1,0:T(8,128)(2,1)S(1)} %cross.1), channel_id=1, replica_groups={{16,0,8,24,2,18,10,26,15,23,7,31,3,11,19,27,4,12,25,28,17,13,21,29,6,14..., dimensions={0} | all-to-all | bytes 1048576 | tf_op jit(solution)/shard_map/all_to_all | solution.py:272
  43.3 1.1 %place.1 = bf16[128,2048]{1,0:T(8,128)(2,1)} custom-call(bf16[32,64,128]{2,1,0:T(8,128)(2,1)S(1)} %all_to_all.11.in_ref), custom_call_target="tpu_custom_call" | custom-call | tf_op jit(solution)/shard_map/place/pallas_call | solution.py:273
  (1 shorter events, 0.0 us)
Async XLA Ops:
  0.0 0.9 %copy-start.1 = (bf16[256,512]{1,0:T(8,128)(2,1)S(1)}, bf16[256,512]{1,0:T(8,128)(2,1)}, u32[]{:S(2)}) copy-start(bf16[256,512]{1,0:T(8,128)(2,1)} %records_ref.1) | copy-start | bytes 786436
  1.0 5.3 %collective-permute-start = (bf16[64,512]{1,0:T(8,128)(2,1)S(1)}, bf16[64,512]{1,0:T(8,128)(2,1)S(1)}, u32[]{:S(2)}, u32[]{:S(2)}) collective-permute-start(bf16[64,512]{1,0:T(8,128)(2,1)S(1)} %get-tuple-element.13), channel_id=1, source_target_pairs={{0,1},{1,0},{2,3},{3,2},{4,5},{5,4},{6,7},{7,6},{8,9},{9,8},{10,11... | collective-permute-start | bytes 196616 | tf_op jit(solution)/shard_map/ppermute | solution.py:238
  1.1 5.2 %collective-permute-start.1 = (bf16[64,512]{1,0:T(8,128)(2,1)S(1)}, bf16[64,512]{1,0:T(8,128)(2,1)S(1)}, u32[]{:S(2)}, u32[]{:S(2)}) collective-permute-start(bf16[64,512]{1,0:T(8,128)(2,1)S(1)} %get-tuple-element.14), channel_id=1, source_target_pairs={{0,2},{1,3},{2,0},{3,1},{4,6},{5,7},{6,4},{7,5},{8,10},{9,11},{10,... | collective-permute-start | bytes 196616 | tf_op jit(solution)/shard_map/ppermute | solution.py:238
  3.8 4.0 %collective-permute-start.2 = (bf16[64,512]{1,0:T(8,128)(2,1)S(1)}, bf16[64,512]{1,0:T(8,128)(2,1)S(1)}, u32[]{:S(2)}, u32[]{:S(2)}) collective-permute-start(bf16[64,512]{1,0:T(8,128)(2,1)S(1)} %get-tuple-element.15), channel_id=1, source_target_pairs={{0,3},{1,2},{2,1},{3,0},{4,7},{5,6},{6,5},{7,4},{8,11},{9,10},{10,... | collective-permute-start | bytes 196616 | tf_op jit(solution)/shard_map/ppermute | solution.py:238
  4.5 1.0 %copy-start = (f32[200,512]{1,0:T(8,128)S(1)}, f32[200,512]{1,0:T(8,128)}, u32[]{:S(2)}) copy-start(f32[200,512]{1,0:T(8,128)} %constant.6.clone.rows_ref) | copy-start | bytes 1228804

commit v10 on v8

--- a/solution.py
+++ b/solution.py
@@ -22,8 +22,8 @@
 EXACT = 256
 AXES = ("region", "slab")
 SPECTRA_RANKS = [
-    24, 16, 8, 0, 15, 23, 7, 31, 26, 10, 18, 2, 19, 3, 11, 27,
-    20, 13, 28, 4, 17, 9, 25, 1, 22, 14, 30, 6, 21, 12, 29, 5,
+    16, 8, 24, 0, 15, 23, 7, 31, 26, 10, 18, 2, 19, 11, 27, 3,
+    20, 13, 28, 4, 21, 12, 29, 5, 22, 14, 30, 6, 17, 9, 25, 1,
 ]
 RESULT_RANKS = [
     16, 0, 8, 24, 17, 13, 21, 29, 15, 23, 7, 31, 3, 11, 19, 27,

time: 45.1 us -> 45.1 us (level)
  no operation moved by 1% of the time
where the time goes in v10:
time: 45.1 us; the launch traced here: 44.9 us
  blocking collectives  33 us (73%)
  Pallas kernels  4.83 us (11%)
  starting transfers between devices  2.84 us (6%)
  local copies, waits for them, and re-layouts  1.95 us (4%)
  waiting for transfers between devices  1.49 us (3%)
  other arithmetic  0.69 us (2%)
    all_to_all x1, blocking collectives, by_bins(): lax.all_to_all(blocks, AXES, split_axis=0, concat_axis=0, tiled=True, axi...  16.6 us
    all_to_all x1, blocking collectives, by_bins(): lax.all_to_all(partial, AXES, split_axis=0, concat_axis=0, tiled=True, ax...  16.5 us
    ppermute x3, starting transfers between devices, by_bins(): lax.ppermute(divided[k], 'slab', [(i, i ^ k) for i in range(slabs)])  2.84 us
    unnamed x4, local copies, waits for them, and re-layouts  1.95 us
    pallas_call x1, Pallas kernels, by_bins(): pl.pallas_call(functools.partial(cross_kernel, regions, slabs), out_shape...  1.66 us
    ppermute x3, waiting for transfers between devices, by_bins(): lax.ppermute(divided[k], 'slab', [(i, i ^ k) for i in range(slabs)])  1.49 us
    pallas_call x1, Pallas kernels, by_bins(): pl.pallas_call(spectra_kernel, out_shape=jax.ShapeDtypeStruct((devices *...  1.22 us
    pallas_call x1, Pallas kernels, by_bins(): pl.pallas_call(place_kernel, out_shape=jax.ShapeDtypeStruct((pair_count,...  1.13 us
  transfers between devices with their start and end apart: 3, of which 1 were waited for; matrix products, arithmetic and copies ran while one was open for 2% of the time, Pallas kernels for 2%

profile of v10, /device:TPU:1, one launch (start us, length us, event | category | flops | bytes accessed | tf_op | source)
XLA Modules:
  0.0 44.9 jit_solution(16415064185517444941)
XLA Ops:
  0.0 0.0 copy-start.1
  0.0 0.9 %copy-done.1 = bf16[256,512]{1,0:T(8,128)(2,1)S(1)} copy-done((bf16[256,512]{1,0:T(8,128)(2,1)S(1)}, bf16[256,512]{1,0:T(8,128)(2,1)}, u32[]{:S(2)}) %copy-start.1) | copy-done | bytes 262168
  1.0 0.1 collective-permute-start
  1.1 2.7 %collective-permute-start.1 = (bf16[64,512]{1,0:T(8,128)(2,1)S(1)}, bf16[64,512]{1,0:T(8,128)(2,1)S(1)}, u32[]{:S(2)}, u32[]{:S(2)}) collective-permute-start(bf16[64,512]{1,0:T(8,128)(2,1)S(1)} %get-tuple-element.14), channel_id=1, source_target_pairs={{0,2},{1,3},{2,0},{3,1},{4,6},{5,7},{6,4},{7,5},{8,10},{9,11},{10,... | collective-permute-start | bytes 196616 | tf_op jit(solution)/shard_map/ppermute | solution.py:238
  3.8 0.0 collective-permute-start.2
  3.8 0.7 %fusion.named_ref = s32[1,128]{1,0:T(1,128)S(1)} fusion(s32[128,1]{0,1:T(1,128)} %param.7, s32[128]{0:T(128)} %param.6, s32[128]{0:T(128)} %param.8), kind=kLoop, calls=%fused_computation.1 | loop fusion | flops 512 | bytes 2048 | tf_op jit(solution)/shard_map/reshape | solution.py:252
  4.5 0.0 copy-start
  4.5 1.0 %copy-done = f32[200,512]{1,0:T(8,128)S(1)} copy-done((f32[200,512]{1,0:T(8,128)S(1)}, f32[200,512]{1,0:T(8,128)}, u32[]{:S(2)}) %copy-start) | copy-done | bytes 409624
  5.5 0.8 %prepare.1 = (bf16[4,128]{1,0:T(4,128)(2,1)S(1)}, f32[8,512]{1,0:T(8,128)S(1)}, bf16[2048,512]{1,0:T(8,128)(2,1)S(1)}) custom-call(s32[1,128]{1,0:T(1,128)S(1)} %fusion.named_ref, f32[200,512]{1,0:T(8,128)S(1)} %copy-done), custom_call_target="tpu_custom_call" | custom-call | flops 2097152 | bytes 2097152 | tf_op jit(solution)/shard_map/prepare/pallas_call | solution.py:240
  6.3 0.0 collective-permute-done.refs_1_
  6.3 0.0 collective-permute-done.1.refs_2_
  6.3 1.5 %collective-permute-done.2.refs_3_ = bf16[64,512]{1,0:T(8,128)(2,1)S(1)} collective-permute-done((bf16[64,512]{1,0:T(8,128)(2,1)S(1)}, bf16[64,512]{1,0:T(8,128)(2,1)S(1)}, u32[]{:S(2)}, u32[]{:S(2)}) %collective-permute-start.2) | collective-permute-done | bytes 65568 | tf_op jit(solution)/shard_map/ppermute | solution.py:238
  7.8 1.2 %spectra.1 = bf16[1152,128]{1,0:T(8,128)(2,1)S(1)} custom-call(bf16[64,512]{1,0:T(8,128)(2,1)S(1)} %get-tuple-element.12.refs_0_, bf16[64,512]{1,0:T(8,128)(2,1)S(1)} %collective-permute-done.refs_1_, bf16[64,512]{1,0:T(8,128)(2,1)S(1)} %collective-permute-done.1.refs_2_, bf16[64,512]{1,0:T(8,128)(2,1)S(1)} %collective-permute-done.2.refs_3_, ...), custom_call_target="tpu_custom_call" | custom-call | tf_op jit(solution)/shard_map/spectra/pallas_call | solution.py:253
  9.0 16.6 %all_to_all.10 = bf16[32,9,4,128]{3,2,1,0:T(4,128)(2,1)S(1)} all-to-all(bf16[32,9,4,128]{3,2,1,0:T(4,128)(2,1)S(1)} %bitcast.8), channel_id=1, replica_groups={{16,8,24,0,15,23,7,31,26,10,18,2,19,11,27,3,20,13,28,4,21,12,29,5,22,14..., dimensions={0} | all-to-all | bytes 589824 | tf_op jit(solution)/shard_map/all_to_all | solution.py:262
  25.6 1.7 %cross.1 = bf16[32,64,128]{2,1,0:T(8,128)(2,1)S(1)} custom-call(bf16[1152,128]{1,0:T(8,128)(2,1)S(1)} %bitcast.9), custom_call_target="tpu_custom_call" | custom-call | tf_op jit(solution)/shard_map/cross/pallas_call | solution.py:263
  27.3 16.5 %all_to_all.11.in_ref = bf16[32,64,128]{2,1,0:T(8,128)(2,1)S(1)} all-to-all(bf16[32,64,128]{2,1,0:T(8,128)(2,1)S(1)} %cross.1), channel_id=1, replica_groups={{16,0,8,24,17,13,21,29,15,23,7,31,3,11,19,27,1,9,5,20,2,18,10,26,6,14,2..., dimensions={0} | all-to-all | bytes 1048576 | tf_op jit(solution)/shard_map/all_to_all | solution.py:272
  43.7 1.1 %place.1 = bf16[128,2048]{1,0:T(8,128)(2,1)} custom-call(bf16[32,64,128]{2,1,0:T(8,128)(2,1)S(1)} %all_to_all.11.in_ref), custom_call_target="tpu_custom_call" | custom-call | tf_op jit(solution)/shard_map/place/pallas_call | solution.py:273
  (1 shorter events, 0.0 us)
Async XLA Ops:
  0.0 0.9 %copy-start.1 = (bf16[256,512]{1,0:T(8,128)(2,1)S(1)}, bf16[256,512]{1,0:T(8,128)(2,1)}, u32[]{:S(2)}) copy-start(bf16[256,512]{1,0:T(8,128)(2,1)} %records_ref.1) | copy-start | bytes 786436
  1.0 5.3 %collective-permute-start = (bf16[64,512]{1,0:T(8,128)(2,1)S(1)}, bf16[64,512]{1,0:T(8,128)(2,1)S(1)}, u32[]{:S(2)}, u32[]{:S(2)}) collective-permute-start(bf16[64,512]{1,0:T(8,128)(2,1)S(1)} %get-tuple-element.13), channel_id=1, source_target_pairs={{0,1},{1,0},{2,3},{3,2},{4,5},{5,4},{6,7},{7,6},{8,9},{9,8},{10,11... | collective-permute-start | bytes 196616 | tf_op jit(solution)/shard_map/ppermute | solution.py:238
  1.1 5.2 %collective-permute-start.1 = (bf16[64,512]{1,0:T(8,128)(2,1)S(1)}, bf16[64,512]{1,0:T(8,128)(2,1)S(1)}, u32[]{:S(2)}, u32[]{:S(2)}) collective-permute-start(bf16[64,512]{1,0:T(8,128)(2,1)S(1)} %get-tuple-element.14), channel_id=1, source_target_pairs={{0,2},{1,3},{2,0},{3,1},{4,6},{5,7},{6,4},{7,5},{8,10},{9,11},{10,... | collective-permute-start | bytes 196616 | tf_op jit(solution)/shard_map/ppermute | solution.py:238
  3.8 4.0 %collective-permute-start.2 = (bf16[64,512]{1,0:T(8,128)(2,1)S(1)}, bf16[64,512]{1,0:T(8,128)(2,1)S(1)}, u32[]{:S(2)}, u32[]{:S(2)}) collective-permute-start(bf16[64,512]{1,0:T(8,128)(2,1)S(1)} %get-tuple-element.15), channel_id=1, source_target_pairs={{0,3},{1,2},{2,1},{3,0},{4,7},{5,6},{6,5},{7,4},{8,11},{9,10},{10,... | collective-permute-start | bytes 196616 | tf_op jit(solution)/shard_map/ppermute | solution.py:238
  4.5 1.0 %copy-start = (f32[200,512]{1,0:T(8,128)S(1)}, f32[200,512]{1,0:T(8,128)}, u32[]{:S(2)}) copy-start(f32[200,512]{1,0:T(8,128)} %constant.6.clone.rows_ref) | copy-start | bytes 1228804
